TPU v7x, 32 devices: a whole 2x2x4 slice. The times are simulated.
32 devices in a mesh: dp: 16 (over z, x, core), fsdp: 2 (over y).
Axes of the slice: x: 2, y: 2, z: 4, core: 2. Of those that a mesh axis runs over, the one named last changes fastest.
Arguments:
- clean_in: bfloat16 [32, 384, 768], P(('dp', 'fsdp')), may hold values from -6 to 6
- noise_bits: int32 [32, 384], P(('dp', 'fsdp')), may hold values from 0 to 1, as said below
- mask_vector: bfloat16 [768], P('fsdp'), may hold values from -6 to 6
- gain_attn: bfloat16 [768], P('fsdp'), may hold values from 0.5 to 1.5
- w_qkv: bfloat16 [768, 2304], P('fsdp'), may hold values from -0.21875 to 0.21875
- w_out: bfloat16 [768, 768], P('fsdp'), may hold values from -0.875 to 0.875
- gain_mlp: bfloat16 [768], P('fsdp'), may hold values from 0.5 to 1.5
- w_up: bfloat16 [768, 3072], P('fsdp'), may hold values from -0.21875 to 0.21875
- bias_up: bfloat16 [3072], P('fsdp'), may hold values from -3 to 3
- w_down: bfloat16 [3072, 768], P('fsdp'), may hold values from -0.109375 to 0.109375
- bias_down: bfloat16 [768], P('fsdp'), may hold values from -2 to 2
- out_grad: bfloat16 [32, 768, 768], P(('dp', 'fsdp')), may hold values from -6 to 6
Outputs:
- block_out: bfloat16 [32, 768, 768], P(('dp', 'fsdp'))
- clean_grad: float32 [32, 384, 768], P(('dp', 'fsdp'))
- mask_vector_grad: float32 [768], P('fsdp')
- gain_attn_grad: float32 [768], P('fsdp')
- w_qkv_grad: float32 [768, 2304], P('fsdp')
- w_out_grad: float32 [768, 768], P('fsdp')
- gain_mlp_grad: float32 [768], P('fsdp')
- w_up_grad: float32 [768, 3072], P('fsdp')
- bias_up_grad: float32 [3072], P('fsdp')
- w_down_grad: float32 [3072, 768], P('fsdp')
- bias_down_grad: float32 [768], P('fsdp')
Inputs may be any that keep to these rules, and one draw needn't show every extreme that they name: `noise_bits`: 1 marks a token replaced by mask_vector in the noisy copy; each aligned block of 16 tokens of a sequence is masked at a rate of its own.
All inputs are finite; a program needn't handle non-finite values.
Results may differ from a plain program's by a relative error of at most 0.014.
Values may be sent and summed in bfloat16 or wider, within the bound.
A program may use at most 256 MiB of HBM per device.

v0:
```python
import jax
import jax.numpy as jnp
from jax import lax
from jax.sharding import PartitionSpec as P

D = 768
H = 12
HD = 64
BLOCK = 16


norm_floor = 1e-05
tanh_scale = 0.7978845608028654
cubic_weight = 0.044715
masked_logit = -1000000000.0


def root_mean_normalize(inputs):
    centered = inputs - jnp.mean(inputs, axis=-1, keepdims=True)
    variance = jnp.mean(centered * centered, axis=-1, keepdims=True)
    inverse_norm_value = lax.rsqrt(variance + norm_floor)
    return (centered * inverse_norm_value, inverse_norm_value)


def root_mean_normalize_backward(
    normalized_input_gradient, unit_input_rows, inverse_norm_value, gain_weight
):
    scaled_output = normalized_input_gradient * gain_weight
    return inverse_norm_value * (
        scaled_output
        - jnp.mean(scaled_output, axis=-1, keepdims=True)
        - unit_input_rows * jnp.mean(scaled_output * unit_input_rows, axis=-1, keepdims=True)
    )


def gelu_slope(inputs):
    cubic = inputs * inputs * inputs
    bent = jnp.tanh(tanh_scale * (inputs + cubic_weight * cubic))
    output = 0.5 * inputs * (1.0 + bent)
    slope = 0.5 * (1.0 + bent) + 0.5 * inputs * (1.0 - bent * bent) * tanh_scale * (
        1.0 + 3.0 * cubic_weight * inputs * inputs
    )
    return (output, slope)


def rotary_tables(length, heads, head_size):
    positions = jnp.arange(length).astype(jnp.float32)
    halfway = head_size // 2
    spacing = 10000.0 ** (-2.0 * jnp.arange(halfway).astype(jnp.float32) / head_size)
    angles = positions[:, None] * spacing[None, :]
    angles = jnp.concatenate([angles, angles], axis=1)
    angles = jnp.tile(angles, (2, heads))
    return (jnp.cos(angles), jnp.sin(angles))


def turned(inputs, heads):
    parts = inputs.reshape(inputs.shape[:-1] + (heads, 2, -1))
    return jnp.concatenate([-parts[..., 1:, :], parts[..., :1, :]], axis=-2).reshape(inputs.shape)


def unturned(inputs, heads):
    parts = inputs.reshape(inputs.shape[:-1] + (heads, 2, -1))
    return jnp.concatenate([parts[..., 1:, :], -parts[..., :1, :]], axis=-2).reshape(inputs.shape)


def visible_pairs(length, block):
    row_index = jnp.arange(2 * length)
    is_clean = row_index >= length
    block_of = row_index % length // block
    row_clean = is_clean[:, None]
    col_clean = is_clean[None, :]
    row_block = block_of[:, None]
    col_block = block_of[None, :]
    noisy_side = ~row_clean & (
        ~col_clean & (row_block == col_block) | col_clean & (col_block < row_block)
    )
    clean_side = row_clean & col_clean & (col_block <= row_block)
    return noisy_side | clean_side


def on_device(
    clean_in,
    noise_bits,
    mask_vector,
    gain_attn,
    w_qkv,
    w_out,
    gain_mlp,
    w_up,
    bias_up,
    w_down,
    bias_down,
    out_grad,
):
    shards = (mask_vector, gain_attn, w_qkv, w_out, gain_mlp, w_up, bias_up, w_down, bias_down)
    gathered = (
        lax.all_gather(shards[0], "fsdp", axis=0, tiled=True),
        lax.all_gather(shards[1], "fsdp", axis=0, tiled=True),
        lax.all_gather(shards[2], "fsdp", axis=0, tiled=True),
        lax.all_gather(shards[3], "fsdp", axis=0, tiled=True),
        lax.all_gather(shards[4], "fsdp", axis=0, tiled=True),
        lax.all_gather(shards[5], "fsdp", axis=0, tiled=True),
        lax.all_gather(shards[6], "fsdp", axis=0, tiled=True),
        lax.all_gather(shards[7], "fsdp", axis=0, tiled=True),
        lax.all_gather(shards[8], "fsdp", axis=0, tiled=True),
    )
    (
        mask_full,
        attention_gain_weight,
        qkv_weight,
        out_weight,
        feedforward_gain_weight,
        up_weight,
        up_bias,
        down_weight,
        down_bias,
    ) = gathered
    length = clean_in.shape[1]
    row_count = 2 * length
    score_scale = HD ** (-0.5)
    cosine, sine_table = rotary_tables(length, H, HD)
    visible = visible_pairs(length, BLOCK)
    clean_rows = clean_in[0].astype(jnp.float32)
    masked = noise_bits[0][:, None] == 1
    noisy_rows = jnp.where(masked, mask_full.astype(jnp.float32)[None, :], clean_rows)
    residual_state = jnp.concatenate([noisy_rows, clean_rows], axis=0)
    attention_unit_rows, attention_inverse_norm = root_mean_normalize(residual_state)
    attention_normalized_input = (
        attention_unit_rows * attention_gain_weight.astype(jnp.float32)
    ).astype(jnp.bfloat16)
    joined = jnp.dot(attention_normalized_input, qkv_weight, preferred_element_type=jnp.float32)
    query_pre = joined[:, :D]
    key_pre = joined[:, D : 2 * D]
    queries = (query_pre * cosine + turned(query_pre, H) * sine_table).astype(jnp.bfloat16)
    keys = (key_pre * cosine + turned(key_pre, H) * sine_table).astype(jnp.bfloat16)
    values = joined[:, 2 * D :].astype(jnp.bfloat16)
    query_heads = queries.reshape(row_count, H, HD)
    key_heads = keys.reshape(row_count, H, HD)
    value_heads = values.reshape(row_count, H, HD)

    def masked_logits():
        raw_scores = jnp.einsum(
            "qhd,khd->hqk", query_heads, key_heads, preferred_element_type=jnp.float32
        )
        return jnp.where(visible[None], raw_scores * score_scale, masked_logit)

    logits = masked_logits()
    highest = jnp.max(logits, axis=-1, keepdims=True)
    log_total = highest + jnp.log(jnp.sum(jnp.exp(logits - highest), axis=-1, keepdims=True))
    probs = jnp.exp(logits - log_total).astype(jnp.bfloat16)
    mixed = (
        jnp.einsum("hqk,khd->qhd", probs, value_heads, preferred_element_type=jnp.float32)
        .reshape(row_count, D)
        .astype(jnp.bfloat16)
    )
    post_attention_state = residual_state + jnp.dot(
        mixed, out_weight, preferred_element_type=jnp.float32
    )
    feedforward_unit_rows, feedforward_inverse_norm = root_mean_normalize(post_attention_state)
    feedforward_normalized_input = (
        feedforward_unit_rows * feedforward_gain_weight.astype(jnp.float32)
    ).astype(jnp.bfloat16)
    pre_act = jnp.dot(
        feedforward_normalized_input, up_weight, preferred_element_type=jnp.float32
    ) + up_bias.astype(jnp.float32)
    act_value, act_slope = gelu_slope(pre_act)
    activated = act_value.astype(jnp.bfloat16)
    result = (
        post_attention_state
        + jnp.dot(activated, down_weight, preferred_element_type=jnp.float32)
        + down_bias.astype(jnp.float32)
    )
    block_out = result.astype(jnp.bfloat16)[None]
    regathered = (
        lax.all_gather(shards[0], "fsdp", axis=0, tiled=True),
        lax.all_gather(shards[1], "fsdp", axis=0, tiled=True),
        lax.all_gather(shards[2], "fsdp", axis=0, tiled=True),
        lax.all_gather(shards[3], "fsdp", axis=0, tiled=True),
        lax.all_gather(shards[4], "fsdp", axis=0, tiled=True),
        lax.all_gather(shards[5], "fsdp", axis=0, tiled=True),
        lax.all_gather(shards[6], "fsdp", axis=0, tiled=True),
        lax.all_gather(shards[7], "fsdp", axis=0, tiled=True),
        lax.all_gather(shards[8], "fsdp", axis=0, tiled=True),
    )
    attention_gain_weight = regathered[1]
    qkv_weight = regathered[2]
    out_weight = regathered[3]
    feedforward_gain_weight = regathered[4]
    up_weight = regathered[5]
    down_weight = regathered[7]
    grad_rows = out_grad[0]
    grad_value = grad_rows.astype(jnp.float32)
    d_act = jnp.einsum("te,fe->tf", grad_rows, down_weight, preferred_element_type=jnp.float32)
    d_pre = (d_act * act_slope).astype(jnp.bfloat16)
    normalized_feedforward_gradient = jnp.einsum(
        "tf,df->td", d_pre, up_weight, preferred_element_type=jnp.float32
    )
    feedforward_gain_addend = jnp.sum(
        normalized_feedforward_gradient * feedforward_unit_rows, axis=0
    )
    d_after = grad_value + root_mean_normalize_backward(
        normalized_feedforward_gradient,
        feedforward_unit_rows,
        feedforward_inverse_norm,
        feedforward_gain_weight.astype(jnp.float32),
    )
    d_branch = d_after.astype(jnp.bfloat16)
    d_mixed = jnp.einsum(
        "te,de->td", d_branch, out_weight, preferred_element_type=jnp.float32
    ).astype(jnp.bfloat16)
    mixed_heads = d_mixed.reshape(row_count, H, HD)
    full_probs = jnp.exp(masked_logits() - log_total)
    d_probs = jnp.einsum(
        "qhd,khd->hqk", mixed_heads, value_heads, preferred_element_type=jnp.float32
    )
    d_values = jnp.einsum(
        "hqk,qhd->khd",
        full_probs.astype(jnp.bfloat16),
        mixed_heads,
        preferred_element_type=jnp.float32,
    ).reshape(row_count, D)
    d_scores = (
        score_scale * full_probs * (d_probs - jnp.sum(full_probs * d_probs, axis=-1, keepdims=True))
    ).astype(jnp.bfloat16)
    d_queries = jnp.einsum(
        "hqk,khd->qhd", d_scores, key_heads, preferred_element_type=jnp.float32
    ).reshape(row_count, D)
    d_keys = jnp.einsum(
        "hqk,qhd->khd", d_scores, query_heads, preferred_element_type=jnp.float32
    ).reshape(row_count, D)
    d_joined = jnp.concatenate(
        [
            d_queries * cosine + unturned(d_queries * sine_table, H),
            d_keys * cosine + unturned(d_keys * sine_table, H),
            d_values,
        ],
        axis=1,
    ).astype(jnp.bfloat16)
    normalized_attention_gradient = jnp.einsum(
        "te,de->td", d_joined, qkv_weight, preferred_element_type=jnp.float32
    )
    attention_gain_addend = jnp.sum(normalized_attention_gradient * attention_unit_rows, axis=0)
    d_stream = d_after + root_mean_normalize_backward(
        normalized_attention_gradient,
        attention_unit_rows,
        attention_inverse_norm,
        attention_gain_weight.astype(jnp.float32),
    )
    d_noisy = d_stream[:length]
    clean_grad = d_stream[length:] + jnp.where(masked, 0.0, d_noisy)
    mask_term = jnp.sum(jnp.where(masked, d_noisy, 0.0), axis=0)
    bias_up_term = jnp.sum(d_pre.astype(jnp.float32), axis=0)
    bias_down_term = jnp.sum(grad_value, axis=0)
    terms = (
        mask_term,
        attention_gain_addend,
        jnp.einsum(
            "td,te->de", attention_normalized_input, d_joined, preferred_element_type=jnp.float32
        ),
        jnp.einsum("td,te->de", mixed, d_branch, preferred_element_type=jnp.float32),
        feedforward_gain_addend,
        jnp.einsum(
            "td,tf->df", feedforward_normalized_input, d_pre, preferred_element_type=jnp.float32
        ),
        bias_up_term,
        jnp.einsum("tf,te->fe", activated, grad_rows, preferred_element_type=jnp.float32),
        bias_down_term,
    )
    owned = (
        lax.psum_scatter(
            terms[0].astype(jnp.bfloat16), "fsdp", scatter_dimension=0, tiled=True
        ).astype(jnp.float32),
        lax.psum_scatter(
            terms[1].astype(jnp.bfloat16), "fsdp", scatter_dimension=0, tiled=True
        ).astype(jnp.float32),
        lax.psum_scatter(
            terms[2].astype(jnp.bfloat16), "fsdp", scatter_dimension=0, tiled=True
        ).astype(jnp.float32),
        lax.psum_scatter(
            terms[3].astype(jnp.bfloat16), "fsdp", scatter_dimension=0, tiled=True
        ).astype(jnp.float32),
        lax.psum_scatter(
            terms[4].astype(jnp.bfloat16), "fsdp", scatter_dimension=0, tiled=True
        ).astype(jnp.float32),
        lax.psum_scatter(
            terms[5].astype(jnp.bfloat16), "fsdp", scatter_dimension=0, tiled=True
        ).astype(jnp.float32),
        lax.psum_scatter(
            terms[6].astype(jnp.bfloat16), "fsdp", scatter_dimension=0, tiled=True
        ).astype(jnp.float32),
        lax.psum_scatter(
            terms[7].astype(jnp.bfloat16), "fsdp", scatter_dimension=0, tiled=True
        ).astype(jnp.float32),
        lax.psum_scatter(
            terms[8].astype(jnp.bfloat16), "fsdp", scatter_dimension=0, tiled=True
        ).astype(jnp.float32),
    )
    summed = lax.psum(
        (owned[0], owned[1], owned[2], owned[3], owned[4], owned[5], owned[6], owned[7], owned[8]),
        "dp",
    )
    return (
        block_out,
        clean_grad[None],
        summed[0],
        summed[1],
        summed[2],
        summed[3],
        summed[4],
        summed[5],
        summed[6],
        summed[7],
        summed[8],
    )


def solution(mesh):
    in_specs = (
        P(("dp", "fsdp"), None, None),
        P(("dp", "fsdp"), None),
        P("fsdp"),
        P("fsdp"),
        P("fsdp", None),
        P("fsdp", None),
        P("fsdp"),
        P("fsdp", None),
        P("fsdp"),
        P("fsdp", None),
        P("fsdp"),
        P(("dp", "fsdp"), None, None),
    )
    out_specs = (
        P(("dp", "fsdp"), None, None),
        P(("dp", "fsdp"), None, None),
        P("fsdp"),
        P("fsdp"),
        P("fsdp", None),
        P("fsdp", None),
        P("fsdp"),
        P("fsdp", None),
        P("fsdp"),
        P("fsdp", None),
        P("fsdp"),
    )
    return jax.shard_map(
        on_device, mesh=mesh, in_specs=in_specs, out_specs=out_specs, check_vma=False
    )
```

profile of v0, /device:TPU:1, one launch (start us, length us, event | category | flops | bytes accessed | tf_op | source)
XLA Modules:
  0.0 821.9 jit_solution(5085388729204222132)
XLA Ops:
  45.0 16.2 %all-gather.10.cloned.1.call-done = bf16[768,2304]{1,0:T(8,128)(2,1)} async-done(((bf16[384,2304]{1,0:T(8,128)(2,1)}), bf16[768,2304]{1,0:T(8,128)(2,1)}) %all-gather.10.cloned.1.call-update) | async-done | bytes 3538960 | tf_op jit(solution)/shard_map/all_gather | solution.py:99
  61.2 5.1 fusion.41
  89.6 8.1 add_convert_fusion.1
  102.5 13.2 %fusion = (f32[12,768]{1,0:T(8,128)S(1)}, f32[12,768,768]{1,2,0:T(8,128)}) fusion(pred[768,768]{0,1:T(8,128)(4,1)S(1)} %and_or_fusion, bf16[768,12,64]{0,2,1:T(8,128)(2,1)} %bitcast.99, bf16[768,12,64]{0,2,1:T(8,128)(2,1)} %bitcast.97), kind=kOutput, calls=%fused_computation.5 | convolution fusion | flops 927194112 | bytes 31297536 | tf_op jit(solution)/shard_map/qhd,khd->hqk/dot_general | solution.py:142
  115.7 12.6 %exponential_reduce_fusion = f32[12,768]{1,0:T(8,128)S(1)} fusion(f32[12,768,768]{1,2,0:T(8,128)} %get-tuple-element.85, f32[12,768]{1,0:T(8,128)S(1)} %get-tuple-element.84, pred[768,768]{0,1:T(8,128)(4,1)S(1)} %and_or_fusion), kind=kLoop, calls=%fused_computation.3 | loop fusion | flops 28302336 | bytes 28975104 | tf_op jit(solution)/shard_map/reduce_sum | solution.py:149
  133.5 14.0 %convolution_convert_fusion.6 = bf16[12,64,768]{2,1,0:T(8,128)(2,1)} fusion(bf16[768,12,64]{0,2,1:T(8,128)(2,1)} %bitcast.101, f32[12,768,768]{1,2,0:T(8,128)} %get-tuple-element.85, f32[12,768]{1,0:T(8,128)S(1)} %log_add_fusion, pred[768,768]{0,1:T(8,128)(4,1)S(1)} %and_or_fusion), kind=kOutput, calls=%fused_computation.57 | convolution fusion | flops 934871040 | bytes 31297536 | tf_op jit(solution)/shard_map/hqk,khd->qhd/dot_general | solution.py:152
  152.2 11.3 %fusion.40 = f32[768,3072]{1,0:T(8,128)} fusion(bf16[768,3072]{1,0:T(8,128)(2,1)} %all-gather.14.cloned.1.call-done, f32[768,768]{0,1:T(8,128)} %copy-done.2, f32[768]{0:T(1024)S(1)} %reshape.402, f32[768]{0:T(1024)S(1)} %add_rsqrt_fusion, f32[768]{0:T(1024)S(1)} %broadcast_multiply_fusion.7), kind=kOutput, calls=%fused_computation.122 | convolution fusion | flops 3626237952 | bytes 16524288 | tf_op jit(solution)/shard_map/dot_general | solution.py:163
  163.5 50.4 %all-gather.16.cloned.1.call-done = bf16[3072,768]{1,0:T(8,128)(2,1)} async-done(((bf16[1536,768]{1,0:T(8,128)(2,1)}), bf16[3072,768]{1,0:T(8,128)(2,1)}) %all-gather.16.cloned.1.call-update) | async-done | bytes 4718608 | tf_op jit(solution)/shard_map/all_gather | solution.py:104
  213.9 13.3 %fusion.46 = (bf16[3072]{0:T(1024)(128)(2,1)}, bf16[768,3072]{1,0:T(8,128)(2,1)S(1)}) fusion(f32[768,3072]{1,0:T(8,128)} %fusion.40, f32[3072]{0:T(1024)S(1)} %bitcast.114, bf16[3072,768]{1,0:T(8,128)(2,1)} %all-gather.16.cloned.1.call-done, bf16[1,768,768]{2,1,0:T(8,128)(2,1)} %param.23), kind=kOutput, calls=%fused_computation.128 | convolution fusion | flops 3673420800 | bytes 20072448 | tf_op jit(solution)/shard_map/te,fe->tf/dot_general | solution.py:193
  227.2 4.8 multiply_reduce_fusion.1
  239.6 23.4 %multiply_reduce_fusion = (f32[12,768]{1,0:T(8,128)S(1)}, f32[12,768,768]{1,2,0:T(8,128)}) fusion(f32[12,768,768]{1,2,0:T(8,128)} %get-tuple-element.85, f32[12,768]{1,0:T(8,128)S(1)} %log_add_fusion, pred[768,768]{0,1:T(8,128)(4,1)S(1)} %and_or_fusion, bf16[768,12,64]{0,2,1:T(8,128)(2,1)S(1)} %bitcast.110, bf16[768,12,64]{0,2,1:T(8,128)(2,1)S(1)} %bitcast.102), kind=kOutput, calls=%fused_computation.1 | convolution fusion | flops 941349888 | bytes 59645952 | tf_op jit(solution)/shard_map/qhd,khd->hqk/dot_general | solution.py:213
  263.0 24.3 %multiply_convert_fusion = bf16[12,768,768]{1,2,0:T(8,128)(2,1)} fusion(f32[12,768,768]{1,2,0:T(8,128)} %get-tuple-element.90, f32[12,768,768]{1,2,0:T(8,128)} %get-tuple-element.85, f32[12,768]{1,0:T(8,128)S(1)} %get-tuple-element.89, f32[12,768]{1,0:T(8,128)S(1)} %log_add_fusion, pred[768,768]{0,1:T(8,128)(4,1)S(1)} %and_or_fusion), kind=kLoop, calls=%fused_computation | loop fusion | flops 49545216 | bytes 71442432 | tf_op jit(solution)/shard_map/convert_element_type | solution.py:224
  287.3 11.2 %fusion.48 = f32[12,64,768]{2,1,0:T(8,128)} fusion(bf16[768,12,64]{0,2,1:T(8,128)(2,1)} %bitcast.100, bf16[12,768,768]{1,2,0:T(8,128)(2,1)} %multiply_convert_fusion), kind=kOutput, calls=%fused_computation.130 | convolution fusion | flops 905969664 | bytes 17694720 | tf_op jit(solution)/shard_map/hqk,qhd->khd/dot_general | solution.py:228
  298.5 9.0 %fusion.47 = f32[12,64,768]{2,1,0:T(8,128)} fusion(bf16[768,12,64]{0,2,1:T(8,128)(2,1)S(1)} %bitcast.98, bf16[12,768,768]{1,2,0:T(8,128)(2,1)} %multiply_convert_fusion), kind=kOutput, calls=%fused_computation.129 | convolution fusion | flops 905969664 | bytes 17694720 | tf_op jit(solution)/shard_map/hqk,khd->qhd/dot_general | solution.py:225
  315.9 14.4 %convolution_convert_fusion.5 = bf16[12,64,768]{2,1,0:T(8,128)(2,1)} fusion(bf16[768,12,64]{0,2,1:T(8,128)(2,1)S(1)} %bitcast.111, f32[12,768,768]{1,2,0:T(8,128)} %get-tuple-element.85, f32[12,768]{1,0:T(8,128)S(1)} %log_add_fusion, pred[768,768]{0,1:T(8,128)(4,1)S(1)} %and_or_fusion), kind=kOutput, calls=%fused_computation.56 | convolution fusion | flops 934871040 | bytes 31297536 | tf_op jit(solution)/shard_map/hqk,qhd->khd/dot_general | solution.py:216
  330.3 6.5 convolution_convert_fusion
  338.1 11.6 %convolution_convert_fusion.1 = bf16[3072,768]{1,0:T(8,128)(2,1)} fusion(bf16[1,768,768]{2,1,0:T(8,128)(2,1)S(1)} %copy-done.13, f32[768,3072]{1,0:T(8,128)} %fusion.40, f32[3072]{0:T(1024)} %bitcast.112), kind=kOutput, calls=%fused_computation.20 | convolution fusion | flops 3649830912 | bytes 15347712 | tf_op jit(solution)/shard_map/tf,te->fe/dot_general | solution.py:266
  349.8 9.1 %convolution_convert_fusion.2 = bf16[768,3072]{1,0:T(8,128)(2,1)} fusion(bf16[768,3072]{1,0:T(8,128)(2,1)} %copy-done.47, f32[768,768]{0,1:T(8,128)} %copy-done.2, f32[768]{0:T(1024)S(1)} %reshape.402, f32[768]{0:T(1024)S(1)} %add_rsqrt_fusion, f32[768]{0:T(1024)S(1)} %broadcast_multiply_fusion.7), kind=kOutput, calls=%fused_computation.21 | convolution fusion | flops 3628597248 | bytes 11805696 | tf_op jit(solution)/shard_map/td,tf->df/dot_general | solution.py:262
  366.1 11.8 %fusion.16 = bf16[1,768,768]{1,2,0:T(8,128)(2,1)} fusion(f32[768,768]{0,1:T(8,128)} %copy-done.2, bf16[3072,768]{1,0:T(8,128)(2,1)} %all-gather.16.cloned.1.call-done, f32[768]{0:T(1024)} %reshape.404, f32[768,3072]{1,0:T(8,128)} %fusion.40, f32[3072]{0:T(1024)} %bitcast.113), kind=kOutput, calls=%fused_computation.59 | convolution fusion | flops 3649241088 | bytes 17710080 | tf_op jit(solution)/shard_map/dot_general | solution.py:170
  380.3 6.7 multiply_reduce_fusion.2
  389.4 5.0 all-reduce.6
  394.9 52.4 %reduce-scatter.11.cloned.1.call-done = bf16[1536,768]{1,0:T(8,128)(2,1)} async-done(((bf16[3072,768]{1,0:T(8,128)(2,1)}), bf16[1536,768]{1,0:T(8,128)(2,1)}) %reduce-scatter.11.cloned.1.call-update) | async-done | bytes 2359312 | tf_op jit(solution)/shard_map/reduce_scatter | solution.py:291
  447.3 63.0 %reduce-scatter.9.cloned.1.call-done = bf16[384,3072]{1,0:T(8,128)(2,1)} async-done(((bf16[768,3072]{1,0:T(8,128)(2,1)}), bf16[384,3072]{1,0:T(8,128)(2,1)}) %reduce-scatter.9.cloned.1.call-update) | async-done | bytes 2359312 | tf_op jit(solution)/shard_map/reduce_scatter | solution.py:285
  510.3 304.3 %all-reduce.8 = (f32[384]{0:T(512)}, f32[384]{0:T(512)}, f32[384,2304]{1,0:T(8,128)}, f32[384,768]{1,0:T(8,128)}, f32[384]{0:T(512)}, /*index=5*/f32[384,3072]{1...) all-reduce(f32[384]{0:T(512)S(1)} %dynamic-slice_convert_fusion.4, ...), channel_id=1, replica_groups=mesh['dp'=16,'fsdp'=2] {'dp'}, use_global_device_ids=true, to_apply=%region_13.14 | all-reduce | flops 3542016 | bytes 21258240 | tf_op jit(solution)/shard_map/psum | solution.py:298
  (201 shorter events, 103.5 us)
Async XLA Ops:
  7.2 54.0 %all-gather.10.cloned.1.call-start = ((), (), s32[]{:S(2)}) async-start(), calls=%async_computation.4 | async-start | bytes 5308416 | tf_op jit(solution)/shard_map/all_gather | solution.py:99
  7.9 139.6 %all-gather.12.cloned.1.call-start = ((), (), s32[]{:S(2)}) async-start(), calls=%async_computation.5 | async-start | bytes 1769472 | tf_op jit(solution)/shard_map/all_gather | solution.py:100
  8.7 19.6 %copy-start.20 = (bf16[1,384,768]{2,1,0:T(8,128)(2,1)S(1)}, bf16[1,384,768]{2,1,0:T(8,128)(2,1)}, u32[]{:S(2)}) copy-start(bf16[1,384,768]{2,1,0:T(8,128)(2,1)} %param.12) | copy-start | bytes 1769476
  8.7 143.4 %all-gather.14.cloned.1.call-start = ((), (), s32[]{:S(2)}) async-start(), calls=%async_computation.6 | async-start | bytes 7077888 | tf_op jit(solution)/shard_map/all_gather | solution.py:102
  9.5 204.4 %all-gather.16.cloned.1.call-start = ((), (), s32[]{:S(2)}) async-start(), calls=%async_computation.7 | async-start | bytes 7077888 | tf_op jit(solution)/shard_map/all_gather | solution.py:104
  10.0 384.8 %reduce-scatter.7.cloned.1.call-start = ((), (), s32[]{:S(2)}) async-start(), calls=%async_computation.9 | async-start | bytes 1769472 | tf_op jit(solution)/shard_map/reduce_scatter | solution.py:279
  11.3 17.4 %copy-start.35 = (pred[384]{0:T(512)(128)(4,1)}, pred[384]{0:T(512)(128)(4,1)S(1)}, u32[]{:S(2)}) copy-start(pred[384]{0:T(512)(128)(4,1)S(1)} %compare_reduce_fusion) | copy-start | bytes 1156
  18.4 42.8 %copy-start.24 = (f32[768]{0:T(1024)}, f32[768]{0:T(1024)S(1)}, u32[]{:S(2)}) copy-start(f32[768]{0:T(1024)S(1)} %reshape.401) | copy-start | bytes 9220
  29.1 32.1 %copy-start.22 = (f32[768]{0:T(1024)}, f32[768]{0:T(1024)S(1)}, u32[]{:S(2)}) copy-start(f32[768]{0:T(1024)S(1)} %broadcast_multiply_fusion.8) | copy-start | bytes 9220
  30.2 31.0 %copy-start.27 = (f32[768]{0:T(1024)}, f32[768]{0:T(1024)S(1)}, u32[]{:S(2)}) copy-start(f32[768]{0:T(1024)S(1)} %add_rsqrt_fusion.1) | copy-start | bytes 9220
  152.1 61.7 %copy-start.31 = (f32[2,1,1536]{2,1,0:T(1,128)S(1)}, f32[2,1,1536]{2,1,0:T(1,128)}, u32[]{:S(2)}) copy-start(f32[2,1,1536]{2,1,0:T(1,128)} %convert_element_type.184) | copy-start | bytes 36868
  213.9 13.3 %copy-start.3 = (f32[768,768]{0,1:T(8,128)S(1)}, f32[768,768]{0,1:T(8,128)}, u32[]{:S(2)}) copy-start(f32[768,768]{0,1:T(8,128)} %copy-done.2) | copy-start | bytes 7077892
  213.9 13.3 %copy-start.11 = (bf16[768,3072]{1,0:T(8,128)(2,1)S(1)}, bf16[768,3072]{1,0:T(8,128)(2,1)}, u32[]{:S(2)}) copy-start(bf16[768,3072]{1,0:T(8,128)(2,1)} %all-gather.14.cloned.1.call-done) | copy-start | bytes 14155780
  239.6 23.4 %copy-start.14 = (bf16[768,768]{0,1:T(8,128)(2,1)}, bf16[768,768]{0,1:T(8,128)(2,1)S(1)}, u32[]{:S(2)}) copy-start(bf16[768,768]{0,1:T(8,128)(2,1)S(1)} %convolution_convert_fusion.3) | copy-start | bytes 3538948
  307.6 87.3 %reduce-scatter.5.cloned.1.call-start = ((), (), s32[]{:S(2)}) async-start(), calls=%async_computation.8 | async-start | bytes 5308416 | tf_op jit(solution)/shard_map/reduce_scatter | solution.py:276
  315.8 14.5 %copy-start.16 = (bf16[768,768]{0,1:T(8,128)(2,1)}, bf16[768,768]{0,1:T(8,128)(2,1)S(1)}, u32[]{:S(2)}) copy-start(bf16[768,768]{0,1:T(8,128)(2,1)S(1)} %get-tuple-element.70) | copy-start | bytes 3538948
  315.8 14.5 %copy-start.23 = (f32[768]{0:T(1024)S(1)}, f32[768]{0:T(1024)}, u32[]{:S(2)}) copy-start(f32[768]{0:T(1024)} %copy-done.22) | copy-start | bytes 9220
  315.8 14.5 %copy-start.25 = (f32[768]{0:T(1024)S(1)}, f32[768]{0:T(1024)}, u32[]{:S(2)}) copy-start(f32[768]{0:T(1024)} %copy-done.24) | copy-start | bytes 9220
  315.9 14.5 %copy-start.28 = (f32[768]{0:T(1024)S(1)}, f32[768]{0:T(1024)}, u32[]{:S(2)}) copy-start(f32[768]{0:T(1024)} %copy-done.27) | copy-start | bytes 9220
  336.8 110.4 %reduce-scatter.11.cloned.1.call-start = ((), (), s32[]{:S(2)}) async-start(), calls=%async_computation.11 | async-start | bytes 7077888 | tf_op jit(solution)/shard_map/reduce_scatter | solution.py:291
  349.7 160.6 %reduce-scatter.9.cloned.1.call-start = ((), (), s32[]{:S(2)}) async-start(), calls=%async_computation.10 | async-start | bytes 7077888 | tf_op jit(solution)/shard_map/reduce_scatter | solution.py:285
  366.1 14.2 %copy-start.17 = (bf16[768,768]{0,1:T(8,128)(2,1)S(1)}, bf16[768,768]{0,1:T(8,128)(2,1)}, u32[]{:S(2)}) copy-start(bf16[768,768]{0,1:T(8,128)(2,1)} %copy-done.16) | copy-start | bytes 3538948
  366.1 14.2 %copy-start.26 = (f32[768]{0:T(1024)S(1)}, f32[768]{0:T(1024)}, u32[]{:S(2)}) copy-start(f32[768]{0:T(1024)} %copy-done.24) | copy-start | bytes 9220
  366.1 14.2 %copy-start.29 = (f32[768]{0:T(1024)S(1)}, f32[768]{0:T(1024)}, u32[]{:S(2)}) copy-start(f32[768]{0:T(1024)} %copy-done.27) | copy-start | bytes 9220
  (32 other events, 116.9 us)
Sparse Core Ops, SparseCore 0:
  9.6 51.5 all-gather.9
  62.7 22.7 all-gather.11
  87.1 62.6 all-gather.13
  151.2 62.6 all-gather.15
  307.7 21.7 reduce-scatter.6
  337.0 47.6 reduce-scatter.4
  387.0 60.2 reduce-scatter.10
  450.2 60.0 reduce-scatter.8
where the time goes:
time: 831 us; the launch traced here: 822 us
  blocking collectives  327 us (39%)
  waiting for transfers between devices  185 us (22%)
  matrix products  174 us (21%)
  other arithmetic  64.6 us (8%)
  local copies, waits for them, and re-layouts  54.9 us (7%)
  between operations  16.5 us (2%)
    psum x1, blocking collectives, on_device(): lax.psum((owned[0], owned[1], owned[2], owned[3], owned[4], owned[5], own...  304 us
    reduce_scatter x1, waiting for transfers between devices, on_device(): lax.psum_scatter(terms[5].astype(jnp.bfloat16), 'fsdp', scatter_dimension...  63 us
    reduce_scatter x1, waiting for transfers between devices, on_device(): lax.psum_scatter(terms[7].astype(jnp.bfloat16), 'fsdp', scatter_dimension...  52.4 us
    all_gather x1, waiting for transfers between devices, on_device(): lax.all_gather(shards[7], 'fsdp', axis=0, tiled=True)  50.4 us
    convert_element_type x1, other arithmetic, on_device(): d_scores = (score_scale * full_probs * (d_probs - jnp.sum(full_probs * d_...  24.3 us
    dot_general x1, matrix products, on_device(): jnp.einsum('qhd,khd->hqk', mixed_heads, value_heads, preferred_element_ty...  23.4 us
    unnamed x108, local copies, waits for them, and re-layouts  19.7 us
  transfers between devices with their start and end apart: 8, of which 4 were waited for; matrix products, arithmetic and copies ran while one was open for 23% of the time, Pallas kernels for 0%

commit v1 on v0

v1 whole, which is shorter than its diff:
```python
import functools
import math

import jax
import jax.numpy as jnp
import numpy as np
from jax import lax
from jax.experimental import pallas as pl
from jax.experimental.pallas import tpu as pltpu
from jax.sharding import PartitionSpec as P

HD = 64
BLOCK = 16
NORM_FLOOR = 1e-05
TANH_SCALE = 0.7978845608028654
CUBIC = 0.044715
BF = jnp.bfloat16
F32 = jnp.float32
MESH = pl.DeviceIdType.MESH
LOGIT_SCALE = 0.125 * math.log2(math.e)
NN = (((1,), (0,)), ((), ()))
NT = (((1,), (1,)), ((), ()))
TN = (((0,), (0,)), ((), ()))


def dot(a, b, dims=NN):
    return lax.dot_general(a, b, dims, preferred_element_type=F32)


def mo(x, n):
    return pl.multiple_of(x, n)


def normalize(x):
    d = x - jnp.mean(x, axis=-1, keepdims=True)
    inv = lax.rsqrt(jnp.mean(d * d, axis=-1, keepdims=True) + NORM_FLOOR)
    return d * inv, inv


def normalize_backward(g, xhat, inv, gain):
    e = g * gain
    return inv * (
        e
        - jnp.mean(e, axis=-1, keepdims=True)
        - xhat * jnp.mean(e * xhat, axis=-1, keepdims=True)
    )


def layer_kernel(
    nbits,
    clean_h, noise, small_in, cos_r, sin_r, wq_h, wo_h, wu_h, wd_h, og_h,
    out_h, cg_h, fin, oq_h, oo_h, ou_h, od_h,
    small, prow, mcol, mbf, mbb, mbe,
    stream, normed, wq, wo, wu, wd, og,
    qkv, qaug, mixed, aa, nm, act, dpre, xs, xr, daf, db, dm, dks, dsn,
    gd, g1, ryd, ry1, rxd, rx1, rad, ra1, rbd, rb1, red, re1,
    sbuf, srec, ss, rs, ls,
):
    L = 384
    D = 768
    T = 2 * L
    NT3 = L // 128
    d = lax.axis_index("dp")
    f = lax.axis_index("fsdp")
    c = lax.rem(d, 2)
    bits = [lax.rem(lax.div(d, 2 ** (b + 1)), 2) for b in range(nbits)]
    sib = (d + 1 - 2 * c, f)
    ypeer = (d, 1 - f)
    peers = [(d + (1 - 2 * bits[b]) * 2 ** (b + 1), f) for b in range(nbits)]
    u = 2 * bits[1] + bits[0]
    sem = [0]
    lsem = [0]
    ends = []

    def take(n=1):
        k = sem[0]
        sem[0] += n
        return k

    def rc(k, src, dst, dev):
        return pltpu.make_async_remote_copy(
            src_ref=src, dst_ref=dst, send_sem=ss.at[k], recv_sem=rs.at[k],
            device_id=dev, device_id_type=MESH,
        )

    def remote(make, n=1):
        k = take(n)
        fam = lambda i=0: make(k + i, i)
        ends.append((fam, n))
        return fam

    def sent(fam):
        for at, (other_fam, n) in enumerate(ends):
            if other_fam is fam:
                for i in range(n):
                    fam(i).wait_send()
                ends.pop(at)
                return

    def local(src, dst):
        k = lsem[0]
        lsem[0] += 1
        return lambda: pltpu.make_async_copy(src, dst, ls.at[k])

    bar = pltpu.get_barrier_semaphore()
    for dev in [sib, ypeer] + peers:
        pl.semaphore_signal(bar, inc=1, device_id=dev, device_id_type=MESH)

    l_clean = [
        local(clean_h.at[0, pl.ds(128 * i, 128)], stream.at[pl.ds(256 * i + 128, 128)])
        for i in range(NT3)
    ]
    mine = mo(f * L, 128)
    other = mo((1 - f) * L, 128)
    l_wq = [
        local(
            wq_h.at[:, pl.ds(mo(j * D + c * L, 128), L)],
            wq.at[pl.ds(mine, L), pl.ds(j * L, L)],
        )
        for j in range(3)
    ]
    l_wo = local(wo_h, wo.at[pl.ds(mine, L)])
    l_wu = [
        local(
            wu_h.at[:, pl.ds(mo(h * 1536 + c * D, 128), D)],
            wu.at[pl.ds(mine, L), pl.ds(h * D, D)],
        )
        for h in range(2)
    ]
    l_wd = local(wd_h.at[pl.ds(mo(c * D, 128), D)], wd.at[pl.ds(mo(f * D, 128), D)])
    l_og = [
        local(
            og_h.at[0, pl.ds((r % 2) * L + 128 * (r // 2), 128)],
            og.at[pl.ds(128 * r, 128)],
        )
        for r in range(2 * NT3)
    ]
    for cp in l_clean + l_wq:
        cp().start()
    small[pl.ds(f, 1)] = small_in[...][None]

    def y_wq(unit):
        rows = mo(96 * unit, 16)
        return remote(
            lambda k, j: rc(
                k,
                wq_h.at[pl.ds(rows, 96), pl.ds(mo(j * D + c * L, 128), L)],
                wq.at[pl.ds(mo(f * L + rows, 16), 96), pl.ds(j * L, L)],
                ypeer,
            ),
            3,
        )

    yw_q = y_wq(u)
    yw_q2 = y_wq(3 - u)
    y_small = remote(lambda k, i: rc(k, small_in, small.at[f], ypeer))

    def spread(buf, base, unit_rows, unit, dev):
        rows = mo(base + unit_rows * unit, 16)
        return remote(
            lambda k, i: rc(
                k, buf.at[pl.ds(rows, unit_rows)], buf.at[pl.ds(rows, unit_rows)], dev
            )
        )

    xw_q = spread(wq, other, 96, u, peers[0])
    zw_q = spread(wq, other, 96, u, peers[1])
    yw_u = remote(
        lambda k, h: rc(
            k,
            wu_h.at[pl.ds(mo(96 * u, 16), 96), pl.ds(mo(h * 1536 + c * D, 128), D)],
            wu.at[pl.ds(mo(f * L + 96 * u, 16), 96), pl.ds(h * D, D)],
            ypeer,
        ),
        2,
    )
    ux, uz = 2 * bits[1] + 1 - bits[0], 2 * (1 - bits[1]) + bits[0]
    xw_u = spread(wu, other, 96, u, peers[0])
    zw_u = spread(wu, other, 96, u, peers[1])
    xw_u2 = spread(wu, other, 48, 2 * uz, peers[0])
    zw_u2 = spread(wu, other, 48, 2 * ux + 1, peers[1])
    odown = mo((1 - f) * D, 128)
    yw_d = remote(
        lambda k, i: rc(
            k,
            wd_h.at[pl.ds(mo(c * D + 192 * u, 16), 192)],
            wd.at[pl.ds(mo(f * D + 192 * u, 16), 192)],
            ypeer,
        )
    )
    xw_d = spread(wd, odown, 192, u, peers[0])
    zw_d = spread(wd, odown, 192, u, peers[1])
    xw_d2 = spread(wd, odown, 96, 2 * uz, peers[0])
    zw_d2 = spread(wd, odown, 96, 2 * ux + 1, peers[1])
    yw_o = remote(
        lambda k, i: rc(
            k,
            wo_h.at[pl.ds(mo(192 * c + 96 * bits[0], 16), 96)],
            wo.at[pl.ds(mo(f * L + 192 * c + 96 * bits[0], 16), 96)],
            ypeer,
        )
    )
    xw_o = spread(wo, mo(other + 192 * c, 16), 96, bits[0], peers[0])
    sw_o = spread(wo, other, 192, c, sib)

    s_norm = remote(
        lambda k, i: rc(
            k, normed.at[pl.ds(mo(256 * i, 16), 256)],
            normed.at[pl.ds(mo(T + 256 * i, 16), 256)], sib,
        ),
        NT3,
    )
    s_og = remote(lambda k, i: rc(k, og.at[pl.ds(0, T)], og.at[pl.ds(T, T)], sib))

    def mixed_copy(k, i):
        s = 1 - i // 3 if isinstance(i, int) else 1 - lax.div(i, 3)
        p = i % 3 if isinstance(i, int) else lax.rem(i, 3)
        lanes = pl.ds(mo(c * L + 128 * p, 128), 128)
        return rc(
            k, mixed.at[pl.ds(mo(s * T, 16), T), lanes],
            mixed.at[pl.ds(mo((1 - s) * T, 16), T), lanes], sib,
        )

    s_mix = remote(mixed_copy, 6)

    def rows_copy(buf, src0, dst, dst0):
        return remote(
            lambda k, i: rc(
                k, buf.at[pl.ds(mo(src0 + 256 * i, 16), 256)],
                dst.at[pl.ds(mo(dst0 + 256 * i, 16), 256)], sib,
            ),
            NT3,
        )

    s_nm = rows_copy(nm, 0, nm, T)
    s_dn = rows_copy(xs, 0, xr, 0)
    s_db = rows_copy(db, 0, db, T)
    s_bo = rows_copy(xs, 0, xr, 0)
    right = pl.ds(D, D)
    s_da = remote(
        lambda k, i: rc(
            k, dpre.at[pl.ds(mo(256 * i, 16), 256), right],
            dpre.at[pl.ds(mo(T + 256 * i, 16), 256), right], sib,
        ),
        NT3,
    )

    class Chunk:
        pass

    chunks = {}

    def make_chunk(name, g, gbase, nr, l0, nl, recv, rbase, oref, orow, olane, blk):
        ch = Chunk()
        ch.name, ch.nr, ch.blk = name, nr, blk
        lanes = pl.ds(l0, nl)
        ry, rx, ra, rb, re = recv
        offs = [0]
        for j in range(3):
            offs.append(offs[-1] + bits[j] * (nr >> (j + 1)))

        def greg(off, n):
            return g.at[pl.ds(mo(gbase(f) + off, 16), n), lanes]

        def rreg(buf, n):
            return buf.at[pl.ds(rbase * n // 256 if rbase else 0, n), lanes]

        def oreg(off, n):
            return oref.at[pl.ds(mo(orow(c) + off, 16), n), pl.ds(mo(olane(c), 128), nl)]

        ch.y = remote(
            lambda k, i: rc(
                k, g.at[pl.ds(mo(gbase(1 - f), 16), nr), lanes], rreg(ry, nr), ypeer
            )
        )
        recvs = (rx, ra, rb)
        ch.rs = []
        for j in range(3):
            n = nr >> (j + 1)
            ch.rs.append(
                remote(
                    lambda k, i, j=j, n=n: rc(
                        k, greg(offs[j] + (1 - bits[j]) * n, n), rreg(recvs[j], n), peers[j]
                    )
                )
            )
        n3 = nr >> 3
        ch.extra = [
            remote(
                lambda k, i, j=j: rc(k, greg(offs[3], n3), rreg(re.at[j - 3], n3), peers[j])
            )
            for j in range(3, nbits)
        ]
        ch.own = local(greg(offs[3], n3), oreg(offs[3], n3))
        ch.ag2 = remote(
            lambda k, i: rc(k, greg(offs[3], n3), oreg(offs[3], n3), peers[2])
        )
        ch.ag1 = remote(
            lambda k, i: rc(k, oreg(offs[2], nr >> 2), oreg(offs[2], nr >> 2), peers[1])
        )
        ch.ag0 = remote(
            lambda k, i: rc(k, oreg(offs[1], nr >> 1), oreg(offs[1], nr >> 1), peers[0])
        )
        ch.ags = remote(lambda k, i: rc(k, oreg(0, nr), oreg(0, nr), sib))

        def add(off, n, rref):
            step = min(blk, n)
            gr = greg(off, n)

            def body(i, carry):
                sl = pl.ds(mo(i * step, 16), step)
                gr[sl, :] = (gr[sl, :].astype(F32) + rref[sl, :].astype(F32)).astype(BF)
                return carry

            lax.fori_loop(0, n // step, body, 0)

        def e_y():
            ch.y().wait_recv()
            add(0, nr, rreg(ry, nr))
            ch.rs[0]().start()

        def e_rs(j):
            ch.rs[j]().wait_recv()
            n = nr >> (j + 1)
            add(offs[j + 1], n, rreg(recvs[j], n))
            if j < 2:
                ch.rs[j + 1]().start()
                return
            for m, fam in enumerate(ch.extra):
                fam().start()
                sent(fam)
                fam().wait_recv()
                add(offs[3], n3, rreg(re.at[m], n3))
            ch.own().start()
            ch.ag2().start()

        def e_ag2():
            ch.own().wait()
            ch.ag2().wait_recv()
            ch.ag1().start()

        def e_ag1():
            ch.ag1().wait_recv()
            ch.ag0().start()

        def e_ag0():
            ch.ag0().wait_recv()
            ch.ags().start()

        def e_end():
            ch.ags().wait_recv()

        ch.events = [e_y, lambda: e_rs(0), lambda: e_rs(1), lambda: e_rs(2), e_ag2, e_ag1, e_ag0, e_end]
        chunks[name] = ch
        return ch

    zero = lambda x: 0
    recv_d = (ryd, rxd, rad, rbd, red)
    recv_1 = (ry1, rx1, ra1, rb1, re1)
    for k in range(3):
        make_chunk(
            f"d{k}", gd, lambda h, k=k: h * D + 256 * k, 256, 0, D, recv_d, 256 * k,
            od_h, lambda core, k=k: core * D + 256 * k, zero, 32,
        )
    for t in range(6):
        make_chunk(
            f"u{t}", g1, lambda h: h * L, L, 256 * t, 256, recv_1, 0,
            ou_h, zero, lambda core, t=t: (t // 3) * 1536 + core * D + (t % 3) * 256, 96,
        )
    for j in range(3):
        make_chunk(
            f"q{j}", g1, lambda h: h * L, L, 1536 + L * j, L, recv_1, 0,
            oq_h, zero, lambda core, j=j: j * D + core * L, 48,
        )
    make_chunk(
        "o", g1, lambda h: h * L, L, 1536 + 3 * L, L, recv_1, 0,
        oo_h, zero, lambda core: core * L, 48,
    )

    def event(name, stage):
        return chunks[name].events[stage]

    pl.semaphore_wait(bar, 2 + nbits)
    y_small().start()
    for j in range(3):
        yw_q(j).start()
    for j in range(3):
        yw_q2(j).start()
    for h in range(2):
        yw_u(h).start()
    yw_o().start()
    yw_d().start()
    for cp in l_og + l_wu + [l_wo, l_wd]:
        cp().start()

    lane = lax.broadcasted_iota(jnp.int32, (1, 128), 1)
    low_half = lane < HD
    rot_low = lax.rem(lane, HD) < HD // 2
    bm = [jnp.where(low_half, 1.0, 0.0).astype(BF), jnp.where(low_half, 0.0, 1.0).astype(BF)]
    selm = [low_half, lane >= HD]
    spare = [HD, 0]
    ir = lax.div(lax.broadcasted_iota(jnp.int32, (128, 128), 0), BLOCK)
    ic = lax.div(lax.broadcasted_iota(jnp.int32, (128, 128), 1), BLOCK)
    neg = -1e30
    mbf[0:128, :] = jnp.where(ic < ir, 0.0, neg)
    mbf[128:256, :] = jnp.where(ic <= ir, 0.0, neg)
    mbb[:, 0:128] = jnp.where(ir < ic, 0.0, neg)
    mbb[:, 128:256] = jnp.where(ir <= ic, 0.0, neg)
    mbe[...] = jnp.where(ir == ic, 0.0, neg)
    nf = noise[...].astype(F32)
    for i in range(NT3):
        mcol[128 * i : 128 * i + 128, :] = jnp.broadcast_to(
            nf[:, 128 * i : 128 * i + 128], (128, 128)
        ).T
    sbuf[0] = jnp.zeros((8, D), F32)

    y_small().wait_recv()
    prow[:, 0:L] = small[0]
    prow[:, L:D] = small[1]
    mvec = prow[0:1, :]
    gain_a = prow[1:2, :]
    gain_m = prow[2:3, :]
    bias_d = prow[3:4, :]
    bias_u = jnp.concatenate(
        [small[h, pl.ds(4 + 2 * c + r, 1), :] for h in range(2) for r in range(2)], axis=1
    )

    def wide(m):
        return jnp.concatenate([m] * (D // 128), axis=1)

    for i in range(NT3):
        l_clean[i]().wait()

    def attn_norm(i, carry):
        n0 = mo(256 * i, 128)
        x = stream[pl.ds(n0 + 128, 128), :].astype(F32)
        m = wide(mcol[pl.ds(mo(128 * i, 128), 128), :])
        y = jnp.where(m > 0.5, mvec, x)
        stream[pl.ds(n0, 128), :] = y.astype(BF)
        normed[pl.ds(n0, 128), :] = (normalize(y)[0] * gain_a).astype(BF)
        normed[pl.ds(n0 + 128, 128), :] = (normalize(x)[0] * gain_a).astype(BF)
        s_norm(i).start()
        return carry

    lax.fori_loop(0, NT3, attn_norm, 0)

    for j in range(3):
        l_wq[j]().wait()
        yw_q(j).wait_recv()
    xw_q().start()
    zw_q().start()
    for i in range(NT3):
        s_norm(i).wait_recv()
    for cp in l_og:
        cp().wait()
    s_og().start()
    for j in range(3):
        yw_q2(j).wait_recv()
    xw_q().wait_recv()
    zw_q().wait_recv()

    def turn(x, cos, sin):
        return x * cos + jnp.where(rot_low, pltpu.roll(x, 96, 1), pltpu.roll(x, 32, 1)) * sin

    def rows2(tab, i):
        t = tab[pl.ds(mo(128 * i, 128), 128), :]
        return jnp.concatenate([t, t], axis=0)

    def qkv_rows(r, carry):
        rows = pl.ds(mo(256 * r, 128), 256)
        joined = dot(normed[rows, :], wq[...])
        i = lax.rem(r, NT3)
        cos, sin = rows2(cos_r, i), rows2(sin_r, i)
        for p in range(6):
            x = joined[:, 128 * p : 128 * p + 128]
            qkv[rows, 128 * p : 128 * p + 128] = turn(x, cos, sin).astype(BF)
        qkv[rows, 2 * L : 3 * L] = joined[:, 2 * L : 3 * L].astype(BF)
        return carry

    lax.fori_loop(0, 2 * NT3, qkv_rows, 0)
    for h in range(2):
        l_wu[h]().wait()
        yw_u(h).wait_recv()
    xw_u().start()
    zw_u().start()

    def run_at(idx, table):
        for k, fns in table.items():
            def go(fns=fns):
                for fn in fns:
                    fn()
            pl.when(idx == k)(go)

    def w_o_1():
        l_wo().wait()
        yw_o().wait_recv()
        xw_o().start()

    def w_u_2():
        xw_u().wait_recv()
        zw_u().wait_recv()
        xw_u2().start()
        zw_u2().start()

    def w_o_2():
        xw_o().wait_recv()
        sw_o().start()

    def w_d_1():
        l_wd().wait()
        yw_d().wait_recv()
        xw_d().start()
        zw_d().start()

    def w_d_2():
        xw_d().wait_recv()
        zw_d().wait_recv()
        xw_d2().start()
        zw_d2().start()

    fwd_events = {2: [w_o_1], 3: [w_u_2, w_o_2], 4: [w_d_1]}

    def attn_fwd(n, carry):
        s, p = 1 - lax.div(n, 3), lax.rem(n, 3)
        r0 = s * T
        lq = pl.ds(mo(128 * p, 128), 128)
        lk = pl.ds(mo(L + 128 * p, 128), 128)
        lv = pl.ds(mo(2 * L + 128 * p, 128), 128)

        def rws(a, m):
            return pl.ds(mo(r0 + a, 128), m)

        for i in range(NT3):
            res = []
            for a in range(2):
                q = qkv[rws(256 * i, 256), lq] * bm[a]
                kc = jnp.concatenate(
                    [qkv[rws(256 * j + 128, 128), lk] for j in range(i + 1)], axis=0
                )
                vc = jnp.concatenate(
                    [qkv[rws(256 * j + 128, 128), lv] for j in range(i + 1)], axis=0
                ) * bm[a] + bm[1 - a]
                vn = qkv[rws(256 * i, 128), lv] * bm[a] + bm[1 - a]
                s1 = dot(q, kc, NT) * LOGIT_SCALE
                sn = dot(q[:128], qkv[rws(256 * i, 128), lk], NT) * LOGIT_SCALE + mbe[...]
                last = s1[:, 128 * i :] + mbf[...]
                s1 = last if i == 0 else jnp.concatenate([s1[:, : 128 * i], last], axis=1)
                m1 = jnp.max(s1, axis=1, keepdims=True)
                mn = jnp.maximum(m1[:128], jnp.max(sn, axis=1, keepdims=True))
                m = jnp.concatenate([mn, m1[128:]], axis=0)
                p1 = jnp.exp2(s1 - m).astype(BF)
                pn = jnp.exp2(sn - mn).astype(BF)
                o = dot(p1, vc)
                o = jnp.concatenate([o[:128] + dot(pn, vn), o[128:]], axis=0)
                val = (m + jnp.log2(o)) * (-1.0 / LOGIT_SCALE)
                hi = val.astype(BF).astype(F32)
                mid = (val - hi).astype(BF).astype(F32)
                lo = val - hi - mid
                extra = jnp.where(
                    lane == spare[a], hi,
                    jnp.where(lane == spare[a] + 1, mid, jnp.where(lane == spare[a] + 2, lo, 0.0)),
                )
                qaug[rws(256 * i, 256), pl.ds(mo(256 * p + 128 * a, 128), 128)] = jnp.where(
                    selm[a], q.astype(F32), extra
                ).astype(BF)
                res.append(o)
            data = jnp.where(low_half, res[0], res[1])
            sums = pltpu.roll(jnp.where(low_half, res[1], res[0]), HD, 1)
            mixed[rws(256 * i, 256), pl.ds(mo(c * L + 128 * p, 128), 128)] = (
                data * (1.0 / sums)
            ).astype(BF)
        s_mix(n).start()
        run_at(n, fwd_events)
        return carry

    lax.fori_loop(0, 6, attn_fwd, 0)

    sw_o().wait_recv()
    for n in range(3):
        s_mix(n).wait_recv()

    def out_proj(i, carry):
        rows = pl.ds(mo(256 * i, 128), 256)
        x = stream[rows, :].astype(F32) + dot(mixed[rows, :], wo[...])
        aa[rows, :] = x
        nm[rows, :] = (normalize(x)[0] * gain_m).astype(BF)
        s_nm(i).start()
        return carry

    lax.fori_loop(0, NT3, out_proj, 0)
    xw_u2().wait_recv()
    zw_u2().wait_recv()
    s_og().wait_recv()
    for i in range(NT3):
        s_nm(i).wait_recv()

    def loop_a(n, carry):
        odd = lax.rem(n, 2)
        h = (1 - f) * (1 - odd) + f * odd
        t = 3 * h + lax.div(n, 2)
        lanes = pl.ds(mo(256 * t, 128), 256)
        bu = jnp.zeros((1, 256), F32)
        for tt in range(6):
            bu = jnp.where(t == tt, bias_u[:, 256 * tt : 256 * tt + 256], bu)

        def rows_a(r, carry):
            rows = pl.ds(mo(512 * r, 128), 512)
            pre = dot(nm[rows, :], wu[:, lanes]) + bu
            sq = pre * pre
            half = 0.5 + 0.5 * jnp.tanh(pre * (TANH_SCALE + TANH_SCALE * CUBIC * sq))
            a = pre * half
            act[rows, lanes] = a.astype(BF)
            slope = half + 2.0 * a * (1.0 - half) * (
                TANH_SCALE + 3.0 * CUBIC * TANH_SCALE * sq
            )
            dpre[rows, lanes] = slope.astype(BF)
            return carry

        lax.fori_loop(0, 3, rows_a, 0)
        gd[pl.ds(mo(256 * t, 128), 256), :] = dot(act[:, lanes], og[...], TN).astype(BF)
        for k in range(3):
            pl.when(n == 2 * k)(lambda k=k: chunks[f"d{k}"].y().start())
        run_at(n, {0: [w_d_2]})
        return carry

    lax.fori_loop(0, 6, loop_a, 0)
    xw_d2().wait_recv()
    zw_d2().wait_recv()

    def loop_b(t, carry):
        lanes = pl.ds(mo(256 * t, 128), 256)

        def rows_b(r, tot):
            rows = pl.ds(mo(512 * r, 128), 512)
            g = dot(og[rows, :], wd[lanes, :], NT) * dpre[rows, lanes].astype(F32)
            dpre[rows, lanes] = g.astype(BF)
            return tot + jnp.sum(g, axis=0, keepdims=True)

        tot = lax.fori_loop(0, 3, rows_b, jnp.zeros((1, 256), F32))
        for tt in range(6):
            def put(tt=tt):
                sbuf[0, 4 + tt // 3 : 5 + tt // 3, 256 * (tt % 3) : 256 * (tt % 3) + 256] = tot
            pl.when(t == tt)(put)
        run_at(t, ev["b"])
        return carry

    ev = {
        "b": {1: [event("d0", 0)], 3: [event("d0", 1)], 5: [event("d0", 2), event("d1", 0)]},
        "u0": [event("d0", 3), event("d1", 1)],
        "u1": [event("d0", 4), event("d1", 2), event("d2", 0)],
        "dn": [event("d0", 5), event("d1", 3), event("d2", 1), event("u0", 0)],
        "dm": [event("d0", 6), event("d1", 4), event("d2", 2), event("u1", 0), event("u0", 1)],
        "att": {
            0: [event("d1", 5), event("d2", 3), event("u2", 0), event("u0", 2), event("u1", 1)],
            1: [event("d1", 6), event("d2", 4), event("u3", 0), event("u0", 3), event("u1", 2), event("u2", 1)],
            2: [event("d2", 5), event("u4", 0), event("u0", 4), event("u1", 3), event("u2", 2), event("u3", 1)],
            3: [event("d2", 6), event("u5", 0), event("u0", 5), event("u1", 4), event("u2", 3), event("u3", 2), event("u4", 1)],
            4: [event("u0", 6), event("u1", 5), event("u2", 4), event("u3", 3), event("u4", 2), event("u5", 1)],
            5: [event("o", 0), event("u1", 6), event("u2", 5), event("u3", 4), event("u4", 3), event("u5", 2)],
        },
        "qg": [event("o", 1), event("u2", 6), event("u3", 5), event("u4", 4), event("u5", 3)],
        "da": [event("q0", 0), event("o", 2), event("u3", 6), event("u4", 5), event("u5", 4)],
        "bo": [event("q1", 0), event("q0", 1), event("o", 3), event("u4", 6), event("u5", 5)],
    }
    tail = [
        event("q2", 0), event("q1", 1), event("q0", 2), event("o", 4), event("u5", 6),
        event("q2", 1), event("q1", 2), event("q0", 3), event("o", 5),
        event("q2", 2), event("q1", 3), event("q0", 4), event("o", 6),
        event("q2", 3), event("q1", 4), event("q0", 5),
        event("q2", 4), event("q1", 5), event("q0", 6),
        event("q2", 5), event("q1", 6), event("q2", 6),
    ] + [ch.events[7] for ch in chunks.values()]

    def handle(key):
        for fn in ev[key]:
            fn()

    lax.fori_loop(0, 6, loop_b, 0)

    for h in range(2):
        g1[:, h * D : h * D + D] = dot(nm[...], dpre[:, h * D : h * D + D], TN).astype(BF)
        for t in range(3 * h, 3 * h + 3):
            chunks[f"u{t}"].y().start()
        handle(f"u{h}")

    def dn_other(i, carry):
        x = dot(dpre[pl.ds(mo(T + 256 * i, 128), 256), :], wu[...], NT)
        xs[pl.ds(mo(256 * i, 128), 256), :] = x.astype(BF)
        s_dn(i).start()
        return carry

    lax.fori_loop(0, NT3, dn_other, 0)

    def dn_own(i, sums):
        rows = pl.ds(mo(256 * i, 128), 256)
        g = dot(dpre[rows, :], wu[...], NT)
        s_dn(i).wait_recv()
        g = g + xr[rows, :].astype(F32)
        xhat, inv = normalize(aa[rows, :])
        ograd = og[rows, :].astype(F32)
        after = ograd + normalize_backward(g, xhat, inv, gain_m)
        daf[rows, :] = after
        db[rows, :] = after.astype(BF)
        s_db(i).start()
        return (
            sums[0] + jnp.sum(g * xhat, axis=0, keepdims=True),
            sums[1] + jnp.sum(ograd, axis=0, keepdims=True),
        )

    zrow = jnp.zeros((1, D), F32)
    g_gain_m, g_bias_d = lax.fori_loop(0, NT3, dn_own, (zrow, zrow))
    sbuf[0, 2:3, :] = g_gain_m
    sbuf[0, 3:4, :] = g_bias_d
    handle("dn")

    wo_rows = pl.ds(mo(c * L, 128), L)
    dm[0:T, :] = dot(db[0:T, :], wo[wo_rows, :], NT).astype(BF)
    for i in range(NT3):
        s_db(i).wait_recv()
    dm[T : 2 * T, :] = dot(db[T : 2 * T, :], wo[wo_rows, :], NT).astype(BF)
    for n in range(3, 6):
        s_mix(n).wait_recv()
    g1[:, 1536 + 3 * L : 1536 + 4 * L] = dot(mixed[...], db[:, wo_rows], TN).astype(BF)
    chunks["o"].y().start()
    handle("dm")

    one_q = [
        jnp.where((lane >= s) & (lane < s + 3), 1.0, 0.0).astype(BF) for s in spare
    ]
    one_d = [
        jnp.where((lane >= s) & (lane < s + 2), 1.0, 0.0).astype(BF) for s in spare
    ]

    def attn_bwd(n, carry):
        s, p = lax.div(n, 3), lax.rem(n, 3)
        r0 = s * T
        lq = pl.ds(mo(128 * p, 128), 128)
        lk = pl.ds(mo(L + 128 * p, 128), 128)
        lv = pl.ds(mo(2 * L + 128 * p, 128), 128)

        def rws(a, m):
            return pl.ds(mo(r0 + a, 128), m)

        dog = dm[rws(0, T), lq]
        prod = dog.astype(F32) * mixed[
            rws(0, T), pl.ds(mo(c * L + 128 * p, 128), 128)
        ].astype(F32)
        doa = []
        for a in range(2):
            val = -jnp.sum(jnp.where(selm[a], prod, 0.0), axis=1, keepdims=True)
            hi = val.astype(BF).astype(F32)
            mid = val - hi
            extra = jnp.where(lane == spare[a], hi, jnp.where(lane == spare[a] + 1, mid, 0.0))
            doa.append(jnp.where(selm[a], dog.astype(F32), extra).astype(BF))
        for kt in range(NT3):
            q0 = 256 * kt
            nq = T - q0
            pts, dss, ptn, dsnn = [], [], [], []
            for a in range(2):
                qa = qaug[rws(q0, nq), pl.ds(mo(256 * p + 128 * a, 128), 128)]
                da = doa[a][q0:]
                kc = qkv[rws(q0 + 128, 128), lk] * bm[a] + one_q[a]
                kn = qkv[rws(q0, 128), lk] * bm[a] + one_q[a]
                vc = qkv[rws(q0 + 128, 128), lv] * bm[a] + one_d[a]
                vn = qkv[rws(q0, 128), lv] * bm[a] + one_d[a]
                st = dot(kc, qa, NT) * LOGIT_SCALE
                first = st[:, :256] + mbb[...]
                st = first if nq == 256 else jnp.concatenate([first, st[:, 256:]], axis=1)
                pt = jnp.exp2(st)
                ds = pt * dot(vc, da, NT)
                dpre[pl.ds(512 * a + 128 * kt, 128), pl.ds(q0, nq)] = ds.astype(BF)
                pts.append(pt.astype(BF))
                dss.append(ds.astype(BF))
                pn = jnp.exp2(dot(kn, qa[:128], NT) * LOGIT_SCALE + mbe[...])
                dn = pn * dot(vn, da[:128], NT)
                dsn[a, kt] = dn.astype(BF)
                ptn.append(pn.astype(BF))
                dsnn.append(dn.astype(BF))
            dom = [dm[rws(q0, nq), lq] * bm[a] for a in range(2)]
            qm = [qkv[rws(q0, nq), lq] * bm[a] for a in range(2)]
            domc, qmc = jnp.concatenate(dom, axis=0), jnp.concatenate(qm, axis=0)
            domn = jnp.concatenate([x[:128] for x in dom], axis=0)
            qmn = jnp.concatenate([x[:128] for x in qm], axis=0)
            dks[pl.ds(q0 + 128, 128), :] = dot(jnp.concatenate(dss, axis=1), qmc)
            dks[pl.ds(q0, 128), :] = dot(jnp.concatenate(dsnn, axis=1), qmn)
            qkv[rws(q0 + 128, 128), lv] = dot(jnp.concatenate(pts, axis=1), domc).astype(BF)
            qkv[rws(q0, 128), lv] = dot(jnp.concatenate(ptn, axis=1), domn).astype(BF)
        for i in range(NT3):
            dq = None
            for a in range(2):
                kc = jnp.concatenate(
                    [qkv[rws(256 * j + 128, 128), lk] for j in range(i + 1)], axis=0
                ) * bm[a]
                part = dot(
                    dpre[pl.ds(512 * a, 128 * (i + 1)), pl.ds(256 * i, 256)], kc, TN
                )
                pn = dot(dsn[a, i], qkv[rws(256 * i, 128), lk] * bm[a], TN)
                part = jnp.concatenate([part[:128] + pn, part[128:]], axis=0)
                dq = part if dq is None else dq + part
            cos, sin = rows2(cos_r, i), rows2(sin_r, i)
            qkv[rws(256 * i, 256), lq] = (turn(dq, cos, -sin) * 0.125).astype(BF)
        for i in range(NT3):
            cos, sin = rows2(cos_r, i), rows2(sin_r, i)
            dk = dks[pl.ds(256 * i, 256), :]
            qkv[rws(256 * i, 256), lk] = (turn(dk, cos, -sin) * 0.125).astype(BF)
        run_at(n, ev["att"])
        return carry

    lax.fori_loop(0, 6, attn_bwd, 0)

    for j in range(3):
        g1[:, 1536 + L * j : 1536 + L * j + L] = dot(
            normed[...], qkv[:, L * j : L * j + L], TN
        ).astype(BF)
        chunks[f"q{j}"].y().start()
    handle("qg")

    def da_other(i, carry):
        x = dot(qkv[pl.ds(mo(T + 256 * i, 128), 256), :], wq[...], NT)
        dpre[pl.ds(mo(256 * i, 128), 256), right] = x.astype(BF)
        s_da(i).start()
        return carry

    lax.fori_loop(0, NT3, da_other, 0)
    cg_out = [
        local(daf.at[pl.ds(256 * i, 128)], cg_h.at[0, pl.ds(128 * i, 128)]) for i in range(NT3)
    ]

    def da_own(i, sums):
        rows = pl.ds(mo(256 * i, 128), 256)
        g = dot(qkv[rows, :], wq[...], NT)
        s_da(i).wait_recv()
        g = g + dpre[pl.ds(mo(T + 256 * i, 128), 256), right].astype(F32)
        xhat, inv = normalize(stream[rows, :].astype(F32))
        ds = daf[rows, :] + normalize_backward(g, xhat, inv, gain_a)
        m = wide(mcol[pl.ds(mo(128 * i, 128), 128), :]) > 0.5
        daf[pl.ds(mo(256 * i, 128), 128), :] = ds[128:] + jnp.where(m, 0.0, ds[:128])
        return (
            sums[0] + jnp.sum(jnp.where(m, ds[:128], 0.0), axis=0, keepdims=True),
            sums[1] + jnp.sum(g * xhat, axis=0, keepdims=True),
        )

    g_mask, g_gain_a = lax.fori_loop(0, NT3, da_own, (zrow, zrow))
    for cp in cg_out:
        cp().start()
    sbuf[0, 0:1, :] = g_mask
    sbuf[0, 1:2, :] = g_gain_a

    smalls = [
        remote(lambda k, i, n=n, dev=dev: rc(k, sbuf.at[n], srec.at[n], dev))
        for n, dev in enumerate([sib, ypeer] + peers)
    ]
    s_last = remote(
        lambda k, i: rc(k, sbuf.at[nbits + 2], srec.at[nbits + 2], sib)
    )
    row = lax.broadcasted_iota(jnp.int32, (8, D), 0)

    def small_step(n):
        smalls[n]().wait_recv()
        new = srec[n]
        if n == 0:
            new = jnp.where(row < 4, new, 0.0)
        sbuf[n + 1] = sbuf[n] + new
        if n + 1 < len(smalls):
            smalls[n + 1]().start()
        else:
            s_last().start()

    smalls[0]().start()
    handle("da")
    small_step(0)

    sent(s_dn)

    def bo_other(i, carry):
        x = dot(act[pl.ds(mo(T + 256 * i, 128), 256), :], wd[...])
        xs[pl.ds(mo(256 * i, 128), 256), :] = x.astype(BF)
        s_bo(i).start()
        return carry

    lax.fori_loop(0, NT3, bo_other, 0)
    small_step(1)
    sent(s_nm)

    def bo_own(i, carry):
        rows = pl.ds(mo(256 * i, 128), 256)
        x = aa[rows, :] + dot(act[rows, :], wd[...])
        s_bo(i).wait_recv()
        nm[rows, :] = (x + xr[rows, :].astype(F32) + bias_d).astype(BF)
        return carry

    lax.fori_loop(0, NT3, bo_own, 0)
    l_out = [
        local(
            nm.at[pl.ds(128 * r, 128)],
            out_h.at[0, pl.ds((r % 2) * L + 128 * (r // 2), 128)],
        )
        for r in range(2 * NT3)
    ]
    for cp in l_out:
        cp().start()
    handle("bo")
    for n in range(2, len(smalls)):
        tail.insert(3 * (n - 1) - 3, lambda n=n: small_step(n))
    for fn in tail:
        fn()
    s_last().wait_recv()
    last = len(smalls)
    tot = sbuf[last]
    oth = srec[last]
    mh = jnp.where(f == 0, tot[0:4, 0:L], tot[0:4, L:D])
    fin[0:4, :] = mh
    for core_off, x in ((c, tot), (1 - c, oth)):
        v = jnp.where(f == 0, x[4:5, :], x[5:6, :])
        fin[pl.ds(4 + 2 * core_off, 1), :] = v[:, 0:L]
        fin[pl.ds(5 + 2 * core_off, 1), :] = v[:, L:D]
    for cp in l_out + cg_out:
        cp().wait()
    for fam, n in list(ends):
        sent(fam)


def tables(length):
    pos = np.arange(length, dtype=np.float32)
    half = HD // 2
    spacing = (10000.0 ** (-2.0 * np.arange(half, dtype=np.float64) / HD)).astype(np.float32)
    ang = (pos[:, None] * spacing[None, :]).astype(np.float64)
    cos = np.tile(np.cos(ang), (1, 4)).astype(np.float32)
    sin = np.sin(ang)
    sin = np.tile(np.concatenate([-sin, sin], axis=1), (1, 2)).astype(np.float32)
    return cos, sin


def on_device(
    nbits, clean_in, noise_bits, mask_vector, gain_attn, w_qkv, w_out, gain_mlp,
    w_up, bias_up, w_down, bias_down, out_grad,
):
    L, D, T = 384, 768, 768
    small = jnp.concatenate(
        [mask_vector, gain_attn, gain_mlp, bias_down, bias_up]
    ).reshape(8, L).astype(F32)
    cos, sin = tables(L)
    nx = max(1, nbits - 3)
    hbm = pl.BlockSpec(memory_space=pltpu.HBM)
    vm = pl.BlockSpec(memory_space=pltpu.VMEM)
    scratch = [
        ((2, 8, L), F32), ((8, D), F32), ((L, 128), F32), ((256, 128), F32),
        ((128, 256), F32), ((128, 128), F32),
        ((T, D), BF), ((2 * T, D), BF), ((D, 1152), BF), ((D, D), BF), ((D, 1536), BF),
        ((1536, D), BF), ((2 * T, D), BF),
        ((2 * T, 1152), BF), ((2 * T, D), BF), ((2 * T, D), BF), ((T, D), F32),
        ((2 * T, D), BF), ((2 * T, 1536), BF), ((2 * T, 1536), BF), ((T, D), BF),
        ((T, D), BF), ((T, D), F32), ((2 * T, D), BF), ((2 * T, L), BF), ((T, 128), F32),
        ((2, 3, 128, 128), BF),
        ((1536, D), BF), ((D, 3072), BF),
        ((D, D), BF), ((L, 3072), BF), ((L, D), BF), ((192, 3072), BF),
        ((192, D), BF), ((96, 3072), BF), ((96, D), BF), ((48, 3072), BF),
        ((nx, 96, D), BF), ((nx, 48, 3072), BF),
        ((nbits + 3, 8, D), F32), ((nbits + 3, 8, D), F32),
    ]
    if nbits == 3:
        scratch[37] = ((1, 16, 128), BF)
        scratch[38] = ((1, 16, 128), BF)
    nsem = 240 + 20 * nx
    outs = pl.pallas_call(
        functools.partial(layer_kernel, nbits),
        out_shape=[
            jax.ShapeDtypeStruct((1, T, D), BF),
            jax.ShapeDtypeStruct((1, L, D), F32),
            jax.ShapeDtypeStruct((8, L), F32),
            jax.ShapeDtypeStruct((L, 2304), BF),
            jax.ShapeDtypeStruct((L, D), BF),
            jax.ShapeDtypeStruct((L, 3072), BF),
            jax.ShapeDtypeStruct((1536, D), BF),
        ],
        in_specs=[hbm, vm, vm, vm, vm, hbm, hbm, hbm, hbm, hbm],
        out_specs=[hbm, hbm, vm, hbm, hbm, hbm, hbm],
        scratch_shapes=[pltpu.VMEM(s, t) for s, t in scratch]
        + [
            pltpu.SemaphoreType.DMA((nsem,)),
            pltpu.SemaphoreType.DMA((nsem,)),
            pltpu.SemaphoreType.DMA((64,)),
        ],
        compiler_params=pltpu.CompilerParams(
            collective_id=0, has_side_effects=True, vmem_limit_bytes=64 * 2**20
        ),
        name="layer",
    )(clean_in, noise_bits, small, cos, sin, w_qkv, w_out, w_up, w_down, out_grad)
    block_out, clean_grad, fin, gq, go, gu, gdn = outs
    return (
        block_out, clean_grad, fin[0], fin[1], gq.astype(F32), go.astype(F32), fin[2],
        gu.astype(F32), fin[4:8].reshape(1536), gdn.astype(F32), fin[3],
    )


def solution(mesh):
    nbits = int(math.log2(mesh.shape["dp"])) - 1
    seq = P(("dp", "fsdp"), None, None)
    row, vec = P("fsdp", None), P("fsdp")
    in_specs = (seq, P(("dp", "fsdp"), None), vec, vec, row, row, vec, row, vec, row, vec, seq)
    out_specs = (seq, seq, vec, vec, row, row, vec, row, vec, row, vec)
    return jax.shard_map(
        functools.partial(on_device, nbits), mesh=mesh,
        in_specs=in_specs, out_specs=out_specs, check_vma=False,
    )
```

time: 831 us -> 210 us (0.25); the launches traced: 822 us -> 210 us
  blocking collectives: 327 us -> 0 us
  Pallas kernels: 0 us -> 188 us
  waiting for transfers between devices: 185 us -> 0 us
  matrix products: 174 us -> 0 us
  other arithmetic: 64.6 us -> 10.2 us
  local copies, waits for them, and re-layouts: 54.9 us -> 10.3 us
  between operations: 16.5 us -> 0.67 us
    psum x1 -> x0, blocking collectives: 304 us -> none  [on_device(): lax.psum((owned[0], owned[1], owned[2], owned[3], owned[4], owned[5], own...]
    pallas_call x0 -> x1, Pallas kernels: none -> 188 us  [on_device(): pl.pallas_call(functools.partial(layer_kernel, nbits), out_shape=[jax.Sha...]
    dot_general x18 -> x0, matrix products: 174 us -> none  [the longest x1 23.4 us: on_device(): jnp.einsum('qhd,khd->hqk', mixed_heads, value_heads, preferred_element_ty...]
    reduce_scatter x4 -> x0, waiting for transfers between devices: 115 us -> none  [the longest x1 63 us: on_device(): lax.psum_scatter(terms[5].astype(jnp.bfloat16), 'fsdp', scatter_dimension...]
    all_gather x4 -> x0, waiting for transfers between devices: 66.6 us -> none  [the longest x1 50.4 us: on_device(): lax.all_gather(shards[7], 'fsdp', axis=0, tiled=True)]
    convert_element_type x14 -> x4, other arithmetic: 33.5 us -> 10.2 us  [the longest x1 4.57 us: on_device(): gu.astype(F32)]
    all_gather x5 -> x0, blocking collectives: 17.5 us -> none  [the longest x1 3.76 us: on_device(): lax.all_gather(shards[8], 'fsdp', axis=0, tiled=True)]
    reduce_sum x6 -> x0, other arithmetic: 13.8 us -> none  [the longest x1 12.6 us: on_device(): jnp.sum(jnp.exp(logits - highest), axis=-1, keepdims=True)]
  transfers between devices with their start and end apart: 8 -> 0, of which waited for: 4 -> 0; matrix products, arithmetic and copies ran while one was open for 23% -> 0% of each run, Pallas kernels for 0% -> 0%
where the time goes in v1:
time: 210 us
  Pallas kernels  188 us (90%)
  local copies, waits for them, and re-layouts  10.3 us (5%)
  other arithmetic  10.2 us (5%)
    pallas_call x1, Pallas kernels, on_device(): pl.pallas_call(functools.partial(layer_kernel, nbits), out_shape=[jax.Sha...  188 us
    unnamed x16, local copies, waits for them, and re-layouts  6.09 us
    convert_element_type x1, other arithmetic, on_device(): gu.astype(F32)  4.57 us

profile of v1, /device:TPU:1, one launch (start us, length us, event | category | flops | bytes accessed | tf_op | source)
XLA Modules:
  0.0 209.7 jit_solution(10592074085733971766)
XLA Ops:
  0.7 0.9 dynamic-update-slice
  1.5 0.9 dynamic-update-slice.1
  2.4 0.9 dynamic-update-slice.2
  3.2 0.9 dynamic-update-slice.3
  4.1 0.9 dynamic-update-slice.4
  5.0 0.6 reshape.29.small_in
  5.6 188.5 %layer.1 = (bf16[1,768,768]{2,1,0:T(8,128)(2,1)}, f32[1,384,768]{2,1,0:T(8,128)}, f32[8,384]{1,0:T(8,128)}, bf16[384,2304]{1,0:T(8,128)(2,1)}, bf16[384,768]{1,0...) custom-call(bf16[1,384,768]{2,1,0:T(8,128)(2,1)} %clean_h.1, s32[1,384]{1,0:T(1,128)} %noise.1, ...), custom_call_target="tpu_custom_call" | custom-call | tf_op jit(solution)/shard_map/layer/pallas_call | solution.py:965
  194.0 1.5 slice_reduce_fusion
  195.5 0.7 slice.18
  196.2 0.6 reshape.28
  196.8 0.0 copy-start
  196.8 4.6 %convert_element_type.21 = f32[384,3072]{1,0:T(8,128)} convert(bf16[384,3072]{1,0:T(8,128)(2,1)} %get-tuple-element.23) | non-fusion elementwise | flops 1179648 | bytes 7077888 | tf_op jit(solution)/shard_map/convert_element_type | solution.py:992
  201.4 0.0 copy-done
  201.4 0.0 copy-start.1
  201.4 2.5 %convert_element_type.22 = f32[1536,768]{1,0:T(8,128)} convert(bf16[1536,768]{1,0:T(8,128)(2,1)S(1)} %copy-done) | non-fusion elementwise | flops 1179648 | bytes 7077888 | tf_op jit(solution)/shard_map/convert_element_type | solution.py:992
  204.0 0.0 copy-done.1
  204.0 0.0 copy-start.4
  204.0 2.0 convert_element_type.19
  206.0 0.0 copy-done.4
  206.0 1.1 convert_element_type.20
  207.1 0.6 copy-done.3
  207.7 1.0 copy.32
  208.7 0.0 copy-done.2
  208.7 1.0 copy.33
  (3 shorter events, 0.0 us)
Async XLA Ops:
  196.8 4.6 %copy-start = (bf16[1536,768]{1,0:T(8,128)(2,1)S(1)}, bf16[1536,768]{1,0:T(8,128)(2,1)}, u32[]{:S(2)}) copy-start(bf16[1536,768]{1,0:T(8,128)(2,1)} %get-tuple-element.24) | copy-start | bytes 7077892
  201.4 2.5 %copy-start.1 = (bf16[384,2304]{1,0:T(8,128)(2,1)S(1)}, bf16[384,2304]{1,0:T(8,128)(2,1)}, u32[]{:S(2)}) copy-start(bf16[384,2304]{1,0:T(8,128)(2,1)} %get-tuple-element.21) | copy-start | bytes 5308420
  204.0 2.0 copy-start.4
  206.0 1.7 copy-start.3
  206.0 2.7 %copy-start.2 = (f32[1,384,768]{2,1,0:T(8,128)S(1)}, f32[1,384,768]{2,1,0:T(8,128)}, u32[]{:S(2)}) copy-start(f32[1,384,768]{2,1,0:T(8,128)} %get-tuple-element.41) | copy-start | bytes 3538948

commit v2 on v1

--- a/solution.py
+++ b/solution.py
@@ -18,9 +18,149 @@
 F32 = jnp.float32
 MESH = pl.DeviceIdType.MESH
 LOGIT_SCALE = 0.125 * math.log2(math.e)
+N_SEND, N_RECV, N_LOCAL = 97, 190, 38
 NN = (((1,), (0,)), ((), ()))
 NT = (((1,), (1,)), ((), ()))
 TN = (((0,), (0,)), ((), ()))
+
+
+ROUTES = {
+    "d0": "0yZ",
+    "d1": "y0Z",
+    "d2": "y0Z",
+    "u0": "0yZ",
+    "u1": "y0Z",
+    "u2": "y012",
+    "u3": "y012",
+    "u4": "y102",
+    "u5": "y012",
+    "q0": "0y12",
+    "q1": "0yZ",
+    "q2": "y0Z",
+    "o": "y102",
+}
+SCHEDULE = {
+    ("u", 0): (
+        ("d1", 0),
+    ),
+    ("u", 1): (
+        ("d0", 0),
+    ),
+    ("dn", 0): (
+        ("d2", 0),
+        ("u0", 0),
+    ),
+    ("dn", 1): (
+        ("u1", 0),
+        ("d1", 1),
+    ),
+    ("dm", 0): (
+        ("u2", 0),
+        ("d2", 1),
+    ),
+    ("att", 0): (
+        ("u1", 1),
+        ("d1", 2),
+        ("u3", 0),
+    ),
+    ("att", 1): (
+        ("u2", 1),
+        ("d2", 2),
+        ("u4", 0),
+    ),
+    ("q", 0): (
+        ("u3", 1),
+        ("u1", 2),
+    ),
+    ("att", 2): (
+        ("u2", 2),
+        ("u5", 0),
+    ),
+    ("att", 3): (
+        ("d1", 3),
+        ("d0", 1),
+    ),
+    ("q", 1): (
+        ("u4", 1),
+        ("d2", 3),
+        ("q0", 0),
+        ("u3", 2),
+        ("u0", 1),
+    ),
+    ("att", 4): (
+        ("u1", 3),
+        ("u5", 1),
+        ("u2", 3),
+    ),
+    ("att", 5): (
+        ("d1", 4),
+        ("o", 0),
+        ("d0", 2),
+        ("u3", 3),
+        ("u5", 2),
+    ),
+    ("q", 2): (
+        ("q0", 1),
+        ("u0", 2),
+    ),
+    ("da", 0): (
+        ("u2", 4),
+        ("q1", 0),
+        ("u4", 2),
+        ("o", 1),
+    ),
+    ("da", 1): (
+        ("d0", 3),
+        ("u3", 4),
+        ("d2", 4),
+        ("u5", 3),
+    ),
+    ("bo", 0): (
+        ("q2", 0),
+        ("q0", 2),
+        ("u1", 4),
+        ("u0", 3),
+        ("o", 2),
+        ("q1", 1),
+        ("u2", 5),
+    ),
+    ("bo", 1): (
+        ("s", 0),
+        ("u4", 3),
+        ("u3", 5),
+        ("u5", 4),
+        ("q0", 3),
+        ("d0", 4),
+    ),
+    "tail": (
+        ("o", 3),
+        ("q2", 1),
+        ("u5", 5),
+        ("q1", 2),
+        ("u0", 4),
+        ("u4", 4),
+        ("q0", 4),
+        ("u2", 6),
+        ("s", 1),
+        ("o", 4),
+        ("u3", 6),
+        ("u5", 6),
+        ("q2", 2),
+        ("q0", 5),
+        ("u4", 5),
+        ("o", 5),
+        ("q1", 3),
+        ("s", 2),
+        ("q0", 6),
+        ("q2", 3),
+        ("u4", 6),
+        ("q1", 4),
+        ("o", 6),
+        ("s", 3),
+        ("q2", 4),
+        ("s", 4),
+    ),
+}
 
 
 def dot(a, b, dims=NN):
@@ -48,12 +188,12 @@
 
 def layer_kernel(
     nbits,
-    clean_h, noise, small_in, cos_r, sin_r, wq_h, wo_h, wu_h, wd_h, og_h,
-    out_h, cg_h, fin, oq_h, oo_h, ou_h, od_h,
-    small, prow, mcol, mbf, mbb, mbe,
+    clean_h, noise, v_mask, v_ga, v_gm, v_bd, v_bu, cos_r, sin_r, wq_h, wo_h, wu_h, wd_h, og_h,
+    out_h, cg_h, fin, o1_h, od_h,
+    small_in, small, prow, mcol, mbf, mbb, mbe,
     stream, normed, wq, wo, wu, wd, og,
     qkv, qaug, mixed, aa, nm, act, dpre, xs, xr, daf, db, dm, dks, dsn,
-    gd, g1, ryd, ry1, rxd, rx1, rad, ra1, rbd, rb1, red, re1,
+    gd, g1, r0d, r01, r1d, r11, r2d, r21, r3d, r31, red, re1,
     sbuf, srec, ss, rs, ls,
 ):
     L = 384
@@ -68,24 +208,28 @@
     ypeer = (d, 1 - f)
     peers = [(d + (1 - 2 * bits[b]) * 2 ** (b + 1), f) for b in range(nbits)]
     u = 2 * bits[1] + bits[0]
-    sem = [0]
-    lsem = [0]
+    send_count, recv_count, local_count = [0], [0], [0]
     ends = []
 
-    def take(n=1):
-        k = sem[0]
-        sem[0] += n
+    def take_send(n):
+        k = send_count[0]
+        send_count[0] += n
+        return k
+
+    def take_recv(n=1):
+        k = recv_count[0]
+        recv_count[0] += n
         return k
 
     def rc(k, src, dst, dev):
         return pltpu.make_async_remote_copy(
-            src_ref=src, dst_ref=dst, send_sem=ss.at[k], recv_sem=rs.at[k],
+            src_ref=src, dst_ref=dst, send_sem=ss.at[k[0]], recv_sem=rs.at[k[1]],
             device_id=dev, device_id_type=MESH,
         )
 
     def remote(make, n=1):
-        k = take(n)
-        fam = lambda i=0: make(k + i, i)
+        k = (take_send(n), take_recv(n))
+        fam = lambda i=0: make((k[0] + i, k[1] + i), i)
         ends.append((fam, n))
         return fam
 
@@ -98,8 +242,8 @@
                 return
 
     def local(src, dst):
-        k = lsem[0]
-        lsem[0] += 1
+        k = local_count[0]
+        local_count[0] += 1
         return lambda: pltpu.make_async_copy(src, dst, ls.at[k])
 
     bar = pltpu.get_barrier_semaphore()
@@ -137,6 +281,10 @@
     ]
     for cp in l_clean + l_wq:
         cp().start()
+    for r, v in enumerate((v_mask, v_ga, v_gm, v_bd)):
+        small_in[r : r + 1, :] = v[...].astype(F32).reshape(1, L)
+    for r in range(4):
+        small_in[4 + r : 5 + r, :] = v_bu[pl.ds(L * r, L)].astype(F32).reshape(1, L)
     small[pl.ds(f, 1)] = small_in[...][None]
 
     def y_wq(unit):
@@ -163,8 +311,19 @@
             )
         )
 
-    xw_q = spread(wq, other, 96, u, peers[0])
-    zw_q = spread(wq, other, 96, u, peers[1])
+
+    def spread_q(dev):
+        rows = mo(other + 96 * u, 16)
+        return remote(
+            lambda k, j: rc(
+                k, wq.at[pl.ds(rows, 96), pl.ds(j * L, L)],
+                wq.at[pl.ds(rows, 96), pl.ds(j * L, L)], dev,
+            ),
+            3,
+        )
+
+    xw_q = spread_q(peers[0])
+    zw_q = spread_q(peers[1])
     yw_u = remote(
         lambda k, h: rc(
             k,
@@ -250,135 +409,175 @@
 
     chunks = {}
 
-    def make_chunk(name, g, gbase, nr, l0, nl, recv, rbase, oref, orow, olane, blk):
+    def make_chunk(name, g, gbase, nr, l0, nl, recv, rbase, oref, orow, blk):
         ch = Chunk()
-        ch.name, ch.nr, ch.blk = name, nr, blk
         lanes = pl.ds(l0, nl)
-        ry, rx, ra, rb, re = recv
-        offs = [0]
-        for j in range(3):
-            offs.append(offs[-1] + bits[j] * (nr >> (j + 1)))
-
-        def greg(off, n):
-            return g.at[pl.ds(mo(gbase(f) + off, 16), n), lanes]
-
-        def rreg(buf, n):
-            return buf.at[pl.ds(rbase * n // 256 if rbase else 0, n), lanes]
-
-        def oreg(off, n):
-            return oref.at[pl.ds(mo(orow(c) + off, 16), n), pl.ds(mo(olane(c), 128), nl)]
-
-        ch.y = remote(
-            lambda k, i: rc(
-                k, g.at[pl.ds(mo(gbase(1 - f), 16), nr), lanes], rreg(ry, nr), ypeer
+        route = ROUTES[name]
+
+        def greg(h, off, n):
+            return g.at[pl.ds(mo(gbase(h) + off, 16), n), lanes]
+
+        def rreg(stage, at, n):
+            return recv[stage].at[pl.ds((rbase >> stage) + at, n), lanes]
+
+        def oreg(core, off, n):
+            return oref.at[core, pl.ds(mo(orow + off, 16), n), lanes]
+
+        def send(copies, before=()):
+            for cp in before:
+                cp().wait_send()
+            for cp in copies:
+                cp().start()
+
+        k_send = take_send(3)
+
+        def copy(i, src, dst, dev):
+            k = take_recv()
+            return lambda: pltpu.make_async_remote_copy(
+                src_ref=src(), dst_ref=dst(), send_sem=ss.at[k_send + i], recv_sem=rs.at[k],
+                device_id=dev, device_id_type=MESH,
             )
-        )
-        recvs = (rx, ra, rb)
-        ch.rs = []
-        for j in range(3):
-            n = nr >> (j + 1)
-            ch.rs.append(
-                remote(
-                    lambda k, i, j=j, n=n: rc(
-                        k, greg(offs[j] + (1 - bits[j]) * n, n), rreg(recvs[j], n), peers[j]
+
+        def add(h, off, n, parts):
+            gr = greg(h, off, n)
+            step = min(blk, n)
+
+            def body(i, carry):
+                sl = pl.ds(mo(i * step, 16), step)
+                x = gr[sl, :].astype(F32)
+                for stage, at in parts:
+                    x = x + rreg(stage, at, n)[sl, :].astype(F32)
+                gr[sl, :] = x.astype(BF)
+                return carry
+
+            lax.fori_loop(0, n // step, body, 0)
+
+        sends, adds, gathers = [], [], []
+        off, n, both, stage = 0, nr, True, 0
+        for step in route:
+            if step == "y":
+                sends.append([copy(
+                    0, lambda off=off, n=n: greg(1 - f, off, n),
+                    lambda stage=stage, n=n: rreg(stage, 0, n), ypeer,
+                )])
+                adds.append([(f, off, n, [(stage, 0)])])
+                both = False
+                stage += 1
+            elif step == "Z":
+                m4 = n // 4
+                out, parts, back = [], [], []
+                where = [(stage, 0), (stage, m4), (stage + 1, 0)]
+                mine_off = off + (2 * bits[1] + bits[2]) * m4
+                for i, (x1, x2) in enumerate(((0, 1), (1, 0), (1, 1))):
+                    b1 = 1 - bits[1] if x1 else bits[1]
+                    b2 = 1 - bits[2] if x2 else bits[2]
+                    dev = (d + (b1 - bits[1]) * 4 + (b2 - bits[2]) * 8, f)
+                    to = off + (2 * b1 + b2) * m4
+                    st, at = where[i]
+                    out.append(copy(
+                        i, lambda to=to, m4=m4: greg(f, to, m4),
+                        lambda st=st, at=at, m4=m4: rreg(st, at, m4), dev,
+                    ))
+                    back.append(dev)
+                    parts.append((st, at))
+                sends.append(out)
+                adds.append([(f, mine_off, m4, parts)])
+                gathers.append((mine_off, m4, back))
+                off, n, stage = mine_off, m4, stage + 2
+            else:
+                j = int(step)
+                m2 = n // 2
+                give, keep = off + (1 - bits[j]) * m2, off + bits[j] * m2
+                owners = [0, 1] if both else [f]
+                sends.append([
+                    copy(
+                        i, lambda h=h, give=give, m2=m2: greg(h, give, m2),
+                        lambda stage=stage, i=i, m2=m2: rreg(stage, i * m2, m2), peers[j],
                     )
-                )
-            )
-        n3 = nr >> 3
-        ch.extra = [
-            remote(
-                lambda k, i, j=j: rc(k, greg(offs[3], n3), rreg(re.at[j - 3], n3), peers[j])
+                    for i, h in enumerate(owners)
+                ])
+                adds.append([(h, keep, m2, [(stage, i * m2)]) for i, h in enumerate(owners)])
+                gathers.append((keep, m2, [peers[j]]))
+                off, n, stage = keep, m2, stage + 1
+        extra = [
+            copy(
+                0, lambda off=off, n=n: greg(f, off, n),
+                lambda j=j, n=n: recv[4].at[j - 3, pl.ds((rbase >> 3), n), lanes], peers[j],
             )
             for j in range(3, nbits)
         ]
-        ch.own = local(greg(offs[3], n3), oreg(offs[3], n3))
-        ch.ag2 = remote(
-            lambda k, i: rc(k, greg(offs[3], n3), oreg(offs[3], n3), peers[2])
-        )
-        ch.ag1 = remote(
-            lambda k, i: rc(k, oreg(offs[2], nr >> 2), oreg(offs[2], nr >> 2), peers[1])
-        )
-        ch.ag0 = remote(
-            lambda k, i: rc(k, oreg(offs[1], nr >> 1), oreg(offs[1], nr >> 1), peers[0])
-        )
-        ch.ags = remote(lambda k, i: rc(k, oreg(0, nr), oreg(0, nr), sib))
-
-        def add(off, n, rref):
-            step = min(blk, n)
-            gr = greg(off, n)
-
-            def body(i, carry):
-                sl = pl.ds(mo(i * step, 16), step)
-                gr[sl, :] = (gr[sl, :].astype(F32) + rref[sl, :].astype(F32)).astype(BF)
-                return carry
-
-            lax.fori_loop(0, n // step, body, 0)
-
-        def e_y():
-            ch.y().wait_recv()
-            add(0, nr, rreg(ry, nr))
-            ch.rs[0]().start()
-
-        def e_rs(j):
-            ch.rs[j]().wait_recv()
-            n = nr >> (j + 1)
-            add(offs[j + 1], n, rreg(recvs[j], n))
-            if j < 2:
-                ch.rs[j + 1]().start()
+        own = local(greg(f, off, n), oreg(c, off, n))
+        back = []
+        for depth, (at, m, devs) in enumerate(reversed(gathers)):
+            back.append([
+                copy(
+                    i,
+                    (lambda at=at, m=m: greg(f, at, m)) if depth == 0
+                    else (lambda at=at, m=m: oreg(c, at, m)),
+                    lambda at=at, m=m: oreg(c, at, m), dev,
+                )
+                for i, dev in enumerate(devs)
+            ])
+        back.append([copy(0, lambda: oreg(c, 0, nr), lambda: oreg(c, 0, nr), sib)])
+
+        def reduce_event(i):
+            for cp in sends[i]:
+                cp().wait_recv()
+            for h, at, m, parts in adds[i]:
+                add(h, at, m, parts)
+            if i + 1 < len(sends):
+                send(sends[i + 1], sends[i])
                 return
-            for m, fam in enumerate(ch.extra):
-                fam().start()
-                sent(fam)
-                fam().wait_recv()
-                add(offs[3], n3, rreg(re.at[m], n3))
-            ch.own().start()
-            ch.ag2().start()
-
-        def e_ag2():
-            ch.own().wait()
-            ch.ag2().wait_recv()
-            ch.ag1().start()
-
-        def e_ag1():
-            ch.ag1().wait_recv()
-            ch.ag0().start()
-
-        def e_ag0():
-            ch.ag0().wait_recv()
-            ch.ags().start()
-
-        def e_end():
-            ch.ags().wait_recv()
-
-        ch.events = [e_y, lambda: e_rs(0), lambda: e_rs(1), lambda: e_rs(2), e_ag2, e_ag1, e_ag0, e_end]
+            send((), sends[i])
+            for m, cp in enumerate(extra):
+                send([cp])
+                send((), [cp])
+                cp().wait_recv()
+                gr = greg(f, off, n)
+                gr[...] = (
+                    gr[...].astype(F32)
+                    + recv[4][m, pl.ds((rbase >> 3), n), lanes].astype(F32)
+                ).astype(BF)
+            own().start()
+            send(back[0])
+
+        def gather_event(i):
+            for cp in back[i]:
+                cp().wait_recv()
+            if i == 0:
+                own().wait()
+            if i + 1 < len(back):
+                send(back[i + 1], back[i])
+            else:
+                send((), back[i])
+
+        ch.start = lambda: send(sends[0])
+        ch.events = [functools.partial(reduce_event, i) for i in range(len(sends))] + [
+            functools.partial(gather_event, i) for i in range(len(back))
+        ]
         chunks[name] = ch
-        return ch
-
-    zero = lambda x: 0
-    recv_d = (ryd, rxd, rad, rbd, red)
-    recv_1 = (ry1, rx1, ra1, rb1, re1)
+
+    recv_d = (r0d, r1d, r2d, r3d, red)
+    recv_1 = (r01, r11, r21, r31, re1)
     for k in range(3):
         make_chunk(
             f"d{k}", gd, lambda h, k=k: h * D + 256 * k, 256, 0, D, recv_d, 256 * k,
-            od_h, lambda core, k=k: core * D + 256 * k, zero, 32,
+            od_h, 256 * k, 32,
         )
     for t in range(6):
-        make_chunk(
-            f"u{t}", g1, lambda h: h * L, L, 256 * t, 256, recv_1, 0,
-            ou_h, zero, lambda core, t=t: (t // 3) * 1536 + core * D + (t % 3) * 256, 96,
-        )
-    for j in range(3):
-        make_chunk(
-            f"q{j}", g1, lambda h: h * L, L, 1536 + L * j, L, recv_1, 0,
-            oq_h, zero, lambda core, j=j: j * D + core * L, 48,
-        )
-    make_chunk(
-        "o", g1, lambda h: h * L, L, 1536 + 3 * L, L, recv_1, 0,
-        oo_h, zero, lambda core: core * L, 48,
-    )
-
-    def event(name, stage):
-        return chunks[name].events[stage]
+        make_chunk(f"u{t}", g1, lambda h: h * L, L, 256 * t, 256, recv_1, 0, o1_h, 0, 48)
+    for p in range(3):
+        make_chunk(f"q{p}", g1, lambda h: h * L, L, 1536 + L * p, L, recv_1, 0, o1_h, 0, 48)
+    make_chunk("o", g1, lambda h: h * L, L, 1536 + 3 * L, L, recv_1, 0, o1_h, 0, 48)
+
+    def handle(key):
+        for name, stage in SCHEDULE.get(key, ()):
+            chunks[name].events[stage]()
+
+    def handle_at(idx, keys):
+        for i, key in keys.items():
+            if SCHEDULE.get(key):
+                pl.when(idx == i)(lambda key=key: handle(key))
 
     pl.semaphore_wait(bar, 2 + nbits)
     y_small().start()
@@ -421,9 +620,6 @@
     gain_a = prow[1:2, :]
     gain_m = prow[2:3, :]
     bias_d = prow[3:4, :]
-    bias_u = jnp.concatenate(
-        [small[h, pl.ds(4 + 2 * c + r, 1), :] for h in range(2) for r in range(2)], axis=1
-    )
 
     def wide(m):
         return jnp.concatenate([m] * (D // 128), axis=1)
@@ -445,19 +641,19 @@
     lax.fori_loop(0, NT3, attn_norm, 0)
 
     for j in range(3):
-        l_wq[j]().wait()
         yw_q(j).wait_recv()
-    xw_q().start()
-    zw_q().start()
+        xw_q(j).start()
+        zw_q(j).start()
     for i in range(NT3):
         s_norm(i).wait_recv()
     for cp in l_og:
         cp().wait()
     s_og().start()
     for j in range(3):
+        l_wq[j]().wait()
         yw_q2(j).wait_recv()
-    xw_q().wait_recv()
-    zw_q().wait_recv()
+        xw_q(j).wait_recv()
+        zw_q(j).wait_recv()
 
     def turn(x, cos, sin):
         return x * cos + jnp.where(rot_low, pltpu.roll(x, 96, 1), pltpu.roll(x, 32, 1)) * sin
@@ -590,21 +786,22 @@
     lax.fori_loop(0, NT3, out_proj, 0)
     xw_u2().wait_recv()
     zw_u2().wait_recv()
-    s_og().wait_recv()
-    for i in range(NT3):
-        s_nm(i).wait_recv()
-
-    def loop_a(n, carry):
-        odd = lax.rem(n, 2)
-        h = (1 - f) * (1 - odd) + f * odd
-        t = 3 * h + lax.div(n, 2)
-        lanes = pl.ds(mo(256 * t, 128), 256)
-        bu = jnp.zeros((1, 256), F32)
-        for tt in range(6):
-            bu = jnp.where(t == tt, bias_u[:, 256 * tt : 256 * tt + 256], bu)
-
-        def rows_a(r, carry):
-            rows = pl.ds(mo(512 * r, 128), 512)
+
+    for n in range(2):
+        h = 1 - f if n == 0 else f
+        lanes = pl.ds(mo(h * D, 128), D)
+        bu = jnp.concatenate(
+            [small[h, pl.ds(4 + 2 * c + r, 1), :] for r in range(2)], axis=1
+        )
+
+        def rows_a(r, carry, n=n, lanes=lanes, bu=bu):
+            if n == 0:
+                @pl.when(r == 2)
+                def _():
+                    for i in range(NT3):
+                        s_nm(i).wait_recv()
+
+            rows = pl.ds(mo(L * r, 128), L)
             pre = dot(nm[rows, :], wu[:, lanes]) + bu
             sq = pre * pre
             half = 0.5 + 0.5 * jnp.tanh(pre * (TANH_SCALE + TANH_SCALE * CUBIC * sq))
@@ -616,72 +813,41 @@
             dpre[rows, lanes] = slope.astype(BF)
             return carry
 
-        lax.fori_loop(0, 3, rows_a, 0)
-        gd[pl.ds(mo(256 * t, 128), 256), :] = dot(act[:, lanes], og[...], TN).astype(BF)
-        for k in range(3):
-            pl.when(n == 2 * k)(lambda k=k: chunks[f"d{k}"].y().start())
-        run_at(n, {0: [w_d_2]})
-        return carry
-
-    lax.fori_loop(0, 6, loop_a, 0)
+        lax.fori_loop(0, 4, rows_a, 0)
+        if n == 0:
+            s_og().wait_recv()
+            w_d_2()
+
+        def down_grad(k, carry, n=n, h=h):
+            at = mo(h * D + 256 * k, 128)
+            gd[pl.ds(at, 256), :] = dot(act[:, pl.ds(at, 256)], og[...], TN).astype(BF)
+            for i in range(3):
+                early = ROUTES[f"d{i}"][0] == "y"
+                if early == (n == 0):
+                    pl.when(k == i)(chunks[f"d{i}"].start)
+            handle_at(k, {i: ("a", n, i) for i in range(3)})
+            return carry
+
+        handle(("a", n))
+        lax.fori_loop(0, 3, down_grad, 0)
     xw_d2().wait_recv()
     zw_d2().wait_recv()
 
-    def loop_b(t, carry):
-        lanes = pl.ds(mo(256 * t, 128), 256)
-
-        def rows_b(r, tot):
-            rows = pl.ds(mo(512 * r, 128), 512)
+    for n in range(2):
+        lanes = pl.ds(n * D, D)
+
+        def rows_b(r, tot, lanes=lanes):
+            rows = pl.ds(mo(L * r, 128), L)
             g = dot(og[rows, :], wd[lanes, :], NT) * dpre[rows, lanes].astype(F32)
             dpre[rows, lanes] = g.astype(BF)
             return tot + jnp.sum(g, axis=0, keepdims=True)
 
-        tot = lax.fori_loop(0, 3, rows_b, jnp.zeros((1, 256), F32))
-        for tt in range(6):
-            def put(tt=tt):
-                sbuf[0, 4 + tt // 3 : 5 + tt // 3, 256 * (tt % 3) : 256 * (tt % 3) + 256] = tot
-            pl.when(t == tt)(put)
-        run_at(t, ev["b"])
-        return carry
-
-    ev = {
-        "b": {1: [event("d0", 0)], 3: [event("d0", 1)], 5: [event("d0", 2), event("d1", 0)]},
-        "u0": [event("d0", 3), event("d1", 1)],
-        "u1": [event("d0", 4), event("d1", 2), event("d2", 0)],
-        "dn": [event("d0", 5), event("d1", 3), event("d2", 1), event("u0", 0)],
-        "dm": [event("d0", 6), event("d1", 4), event("d2", 2), event("u1", 0), event("u0", 1)],
-        "att": {
-            0: [event("d1", 5), event("d2", 3), event("u2", 0), event("u0", 2), event("u1", 1)],
-            1: [event("d1", 6), event("d2", 4), event("u3", 0), event("u0", 3), event("u1", 2), event("u2", 1)],
-            2: [event("d2", 5), event("u4", 0), event("u0", 4), event("u1", 3), event("u2", 2), event("u3", 1)],
-            3: [event("d2", 6), event("u5", 0), event("u0", 5), event("u1", 4), event("u2", 3), event("u3", 2), event("u4", 1)],
-            4: [event("u0", 6), event("u1", 5), event("u2", 4), event("u3", 3), event("u4", 2), event("u5", 1)],
-            5: [event("o", 0), event("u1", 6), event("u2", 5), event("u3", 4), event("u4", 3), event("u5", 2)],
-        },
-        "qg": [event("o", 1), event("u2", 6), event("u3", 5), event("u4", 4), event("u5", 3)],
-        "da": [event("q0", 0), event("o", 2), event("u3", 6), event("u4", 5), event("u5", 4)],
-        "bo": [event("q1", 0), event("q0", 1), event("o", 3), event("u4", 6), event("u5", 5)],
-    }
-    tail = [
-        event("q2", 0), event("q1", 1), event("q0", 2), event("o", 4), event("u5", 6),
-        event("q2", 1), event("q1", 2), event("q0", 3), event("o", 5),
-        event("q2", 2), event("q1", 3), event("q0", 4), event("o", 6),
-        event("q2", 3), event("q1", 4), event("q0", 5),
-        event("q2", 4), event("q1", 5), event("q0", 6),
-        event("q2", 5), event("q1", 6), event("q2", 6),
-    ] + [ch.events[7] for ch in chunks.values()]
-
-    def handle(key):
-        for fn in ev[key]:
-            fn()
-
-    lax.fori_loop(0, 6, loop_b, 0)
-
-    for h in range(2):
-        g1[:, h * D : h * D + D] = dot(nm[...], dpre[:, h * D : h * D + D], TN).astype(BF)
-        for t in range(3 * h, 3 * h + 3):
-            chunks[f"u{t}"].y().start()
-        handle(f"u{h}")
+        sbuf[0, 4 + n : 5 + n, :] = lax.fori_loop(0, 4, rows_b, jnp.zeros((1, D), F32))
+        handle(("b", n))
+        g1[:, n * D : n * D + D] = dot(nm[...], dpre[:, n * D : n * D + D], TN).astype(BF)
+        for t in range(3 * n, 3 * n + 3):
+            chunks[f"u{t}"].start()
+        handle(("u", n))
 
     def dn_other(i, carry):
         x = dot(dpre[pl.ds(mo(T + 256 * i, 128), 256), :], wu[...], NT)
@@ -690,6 +856,7 @@
         return carry
 
     lax.fori_loop(0, NT3, dn_other, 0)
+    handle(("dn", 0))
 
     def dn_own(i, sums):
         rows = pl.ds(mo(256 * i, 128), 256)
@@ -711,7 +878,7 @@
     g_gain_m, g_bias_d = lax.fori_loop(0, NT3, dn_own, (zrow, zrow))
     sbuf[0, 2:3, :] = g_gain_m
     sbuf[0, 3:4, :] = g_bias_d
-    handle("dn")
+    handle(("dn", 1))
 
     wo_rows = pl.ds(mo(c * L, 128), L)
     dm[0:T, :] = dot(db[0:T, :], wo[wo_rows, :], NT).astype(BF)
@@ -721,8 +888,8 @@
     for n in range(3, 6):
         s_mix(n).wait_recv()
     g1[:, 1536 + 3 * L : 1536 + 4 * L] = dot(mixed[...], db[:, wo_rows], TN).astype(BF)
-    chunks["o"].y().start()
-    handle("dm")
+    chunks["o"].start()
+    handle(("dm", 0))
 
     one_q = [
         jnp.where((lane >= s) & (lane < s + 3), 1.0, 0.0).astype(BF) for s in spare
@@ -732,7 +899,7 @@
     ]
 
     def attn_bwd(n, carry):
-        s, p = lax.div(n, 3), lax.rem(n, 3)
+        s, p = lax.rem(n, 2), lax.div(n, 2)
         r0 = s * T
         lq = pl.ds(mo(128 * p, 128), 128)
         lk = pl.ds(mo(L + 128 * p, 128), 128)
@@ -803,17 +970,19 @@
             cos, sin = rows2(cos_r, i), rows2(sin_r, i)
             dk = dks[pl.ds(256 * i, 256), :]
             qkv[rws(256 * i, 256), lk] = (turn(dk, cos, -sin) * 0.125).astype(BF)
-        run_at(n, ev["att"])
+        handle_at(n, {i: ("att", i) for i in range(6)})
+
+        @pl.when(s == 1)
+        def _():
+            dj = jnp.concatenate([qkv[:, lq], qkv[:, lk], qkv[:, lv]], axis=1)
+            g1[:, pl.ds(mo(1536 + L * p, 128), L)] = dot(normed[...], dj, TN).astype(BF)
+
+        for i in range(3):
+            pl.when(n == 2 * i + 1)(chunks[f"q{i}"].start)
+        handle_at(n, {2 * i + 1: ("q", i) for i in range(3)})
         return carry
 
     lax.fori_loop(0, 6, attn_bwd, 0)
-
-    for j in range(3):
-        g1[:, 1536 + L * j : 1536 + L * j + L] = dot(
-            normed[...], qkv[:, L * j : L * j + L], TN
-        ).astype(BF)
-        chunks[f"q{j}"].y().start()
-    handle("qg")
 
     def da_other(i, carry):
         x = dot(qkv[pl.ds(mo(T + 256 * i, 128), 256), :], wq[...], NT)
@@ -822,6 +991,7 @@
         return carry
 
     lax.fori_loop(0, NT3, da_other, 0)
+    handle(("da", 0))
     cg_out = [
         local(daf.at[pl.ds(256 * i, 128)], cg_h.at[0, pl.ds(128 * i, 128)]) for i in range(NT3)
     ]
@@ -866,9 +1036,17 @@
         else:
             s_last().start()
 
+    def small_rest():
+        for n in range(4, len(smalls)):
+            small_step(n)
+
+    small_sum = Chunk()
+    small_sum.events = [functools.partial(small_step, n) for n in range(4)] + [
+        small_rest, lambda: s_last().wait_recv(),
+    ]
+    chunks["s"] = small_sum
     smalls[0]().start()
-    handle("da")
-    small_step(0)
+    handle(("da", 1))
 
     sent(s_dn)
 
@@ -879,7 +1057,7 @@
         return carry
 
     lax.fori_loop(0, NT3, bo_other, 0)
-    small_step(1)
+    handle(("bo", 0))
     sent(s_nm)
 
     def bo_own(i, carry):
@@ -899,12 +1077,10 @@
     ]
     for cp in l_out:
         cp().start()
-    handle("bo")
-    for n in range(2, len(smalls)):
-        tail.insert(3 * (n - 1) - 3, lambda n=n: small_step(n))
-    for fn in tail:
-        fn()
-    s_last().wait_recv()
+    handle(("bo", 1))
+    handle("tail")
+    for ch in chunks.values():
+        ch.events[-1]()
     last = len(smalls)
     tot = sbuf[last]
     oth = srec[last]
@@ -931,20 +1107,74 @@
     return cos, sin
 
 
+def finish_kernel(
+    o1_h, od_h, fin, bo_h, cg_h,
+    gq_h, go_h, gu_h, gd_h, out_h, clean_h, v_mask, v_ga, v_gm, v_bd, v_bu,
+    b1, bd, fq, fo, fu, fd, bo, cg, ls,
+):
+    L, D, NB = 384, 768, 4
+    count = [0]
+
+    def copy(src, dst):
+        k = count[0]
+        count[0] += 1
+        cp = pltpu.make_async_copy(src, dst, ls.at[k])
+        cp.start()
+        return cp
+
+    rows = [pl.ds(L // NB * r, L // NB) for r in range(NB)]
+    in1 = [copy(o1_h.at[:, rows[r]], b1.at[:, rows[r]]) for r in range(NB)]
+    ind = [copy(od_h.at[core], bd.at[core]) for core in range(2)]
+    through = [copy(bo_h, bo), copy(cg_h, cg)]
+    outs = []
+    for r in range(NB):
+        in1[r].wait()
+        for core in range(2):
+            for h in range(2):
+                fu[rows[r], 1536 * h + D * core : 1536 * h + D * core + D] = b1[
+                    core, rows[r], D * h : D * h + D
+                ].astype(F32)
+            for p in range(3):
+                for kind in range(3):
+                    src = 1536 + L * p + 128 * kind
+                    dst = D * kind + L * core + 128 * p
+                    fq[rows[r], dst : dst + 128] = b1[core, rows[r], src : src + 128].astype(F32)
+            fo[rows[r], L * core : L * core + L] = b1[
+                core, rows[r], 1536 + 3 * L : 1536 + 4 * L
+            ].astype(F32)
+        for buf, ref in ((fu, gu_h), (fq, gq_h), (fo, go_h)):
+            outs.append(copy(buf.at[rows[r]], ref.at[rows[r]]))
+        if r < 2:
+            through[r].wait()
+            outs.append(copy((bo, cg)[r], (out_h, clean_h)[r]))
+    for core in range(2):
+        ind[core].wait()
+        for r in range(2):
+            part = slice(L * r, L * r + L)
+            at = D * core + L * r
+            fd[at : at + L, :] = bd[core, part, :].astype(F32)
+            outs.append(copy(fd.at[pl.ds(at, L)], gd_h.at[pl.ds(at, L)]))
+    v_mask[...] = fin[0, :]
+    v_ga[...] = fin[1, :]
+    v_gm[...] = fin[2, :]
+    v_bd[...] = fin[3, :]
+    for r in range(4):
+        v_bu[L * r : L * r + L] = fin[4 + r, :]
+    for cp in outs:
+        cp.wait()
+
+
 def on_device(
     nbits, clean_in, noise_bits, mask_vector, gain_attn, w_qkv, w_out, gain_mlp,
     w_up, bias_up, w_down, bias_down, out_grad,
 ):
     L, D, T = 384, 768, 768
-    small = jnp.concatenate(
-        [mask_vector, gain_attn, gain_mlp, bias_down, bias_up]
-    ).reshape(8, L).astype(F32)
     cos, sin = tables(L)
     nx = max(1, nbits - 3)
     hbm = pl.BlockSpec(memory_space=pltpu.HBM)
     vm = pl.BlockSpec(memory_space=pltpu.VMEM)
     scratch = [
-        ((2, 8, L), F32), ((8, D), F32), ((L, 128), F32), ((256, 128), F32),
+        ((8, L), F32), ((2, 8, L), F32), ((8, D), F32), ((L, 128), F32), ((256, 128), F32),
         ((128, 256), F32), ((128, 128), F32),
         ((T, D), BF), ((2 * T, D), BF), ((D, 1152), BF), ((D, D), BF), ((D, 1536), BF),
         ((1536, D), BF), ((2 * T, D), BF),
@@ -955,42 +1185,60 @@
         ((1536, D), BF), ((D, 3072), BF),
         ((D, D), BF), ((L, 3072), BF), ((L, D), BF), ((192, 3072), BF),
         ((192, D), BF), ((96, 3072), BF), ((96, D), BF), ((48, 3072), BF),
-        ((nx, 96, D), BF), ((nx, 48, 3072), BF),
+        ((nx, 96, D), BF) if nbits > 3 else ((1, 16, 128), BF),
+        ((nx, 48, 3072), BF) if nbits > 3 else ((1, 16, 128), BF),
         ((nbits + 3, 8, D), F32), ((nbits + 3, 8, D), F32),
     ]
-    if nbits == 3:
-        scratch[37] = ((1, 16, 128), BF)
-        scratch[38] = ((1, 16, 128), BF)
-    nsem = 240 + 20 * nx
-    outs = pl.pallas_call(
+    block_out, clean_grad, fin, g1, gd = pl.pallas_call(
         functools.partial(layer_kernel, nbits),
         out_shape=[
             jax.ShapeDtypeStruct((1, T, D), BF),
             jax.ShapeDtypeStruct((1, L, D), F32),
             jax.ShapeDtypeStruct((8, L), F32),
-            jax.ShapeDtypeStruct((L, 2304), BF),
-            jax.ShapeDtypeStruct((L, D), BF),
-            jax.ShapeDtypeStruct((L, 3072), BF),
-            jax.ShapeDtypeStruct((1536, D), BF),
+            jax.ShapeDtypeStruct((2, L, 3072), BF),
+            jax.ShapeDtypeStruct((2, D, D), BF),
         ],
-        in_specs=[hbm, vm, vm, vm, vm, hbm, hbm, hbm, hbm, hbm],
-        out_specs=[hbm, hbm, vm, hbm, hbm, hbm, hbm],
+        in_specs=[hbm] + [vm] * 8 + [hbm] * 5,
+        out_specs=[hbm, hbm, vm, hbm, hbm],
         scratch_shapes=[pltpu.VMEM(s, t) for s, t in scratch]
         + [
-            pltpu.SemaphoreType.DMA((nsem,)),
-            pltpu.SemaphoreType.DMA((nsem,)),
-            pltpu.SemaphoreType.DMA((64,)),
+            pltpu.SemaphoreType.DMA((N_SEND,)),
+            pltpu.SemaphoreType.DMA((N_RECV + 20 * (nx - 1),)),
+            pltpu.SemaphoreType.DMA((N_LOCAL,)),
         ],
         compiler_params=pltpu.CompilerParams(
             collective_id=0, has_side_effects=True, vmem_limit_bytes=64 * 2**20
         ),
         name="layer",
-    )(clean_in, noise_bits, small, cos, sin, w_qkv, w_out, w_up, w_down, out_grad)
-    block_out, clean_grad, fin, gq, go, gu, gdn = outs
-    return (
-        block_out, clean_grad, fin[0], fin[1], gq.astype(F32), go.astype(F32), fin[2],
-        gu.astype(F32), fin[4:8].reshape(1536), gdn.astype(F32), fin[3],
+    )(
+        clean_in, noise_bits, mask_vector, gain_attn, gain_mlp, bias_down, bias_up, cos, sin,
+        w_qkv, w_out, w_up, w_down, out_grad,
     )
+    vec = jax.ShapeDtypeStruct((L,), F32)
+    gq, go, gu, gdown, out, clean, v_mask, v_ga, v_gm, v_bd, v_bu = pl.pallas_call(
+        finish_kernel,
+        out_shape=[
+            jax.ShapeDtypeStruct((L, 2304), F32),
+            jax.ShapeDtypeStruct((L, D), F32),
+            jax.ShapeDtypeStruct((L, 3072), F32),
+            jax.ShapeDtypeStruct((1536, D), F32),
+            jax.ShapeDtypeStruct((1, T, D), BF),
+            jax.ShapeDtypeStruct((1, L, D), F32),
+            vec, vec, vec, vec, jax.ShapeDtypeStruct((4 * L,), F32),
+        ],
+        in_specs=[hbm, hbm, vm, hbm, hbm],
+        out_specs=[hbm] * 6 + [vm] * 5,
+        scratch_shapes=[
+            pltpu.VMEM((2, L, 3072), BF), pltpu.VMEM((2, D, D), BF),
+            pltpu.VMEM((L, 2304), F32), pltpu.VMEM((L, D), F32),
+            pltpu.VMEM((L, 3072), F32), pltpu.VMEM((1536, D), F32),
+            pltpu.VMEM((1, T, D), BF), pltpu.VMEM((1, L, D), F32),
+            pltpu.SemaphoreType.DMA((26,)),
+        ],
+        compiler_params=pltpu.CompilerParams(vmem_limit_bytes=64 * 2**20),
+        name="finish",
+    )(g1, gd, fin, block_out, clean_grad)
+    return out, clean, v_mask, v_ga, gq, go, v_gm, gu, v_bu, gdown, v_bd
 
 
 def solution(mesh):

time: 210 us -> 167 us (0.80)
  Pallas kernels: 188 us -> 166 us
  local copies, waits for them, and re-layouts: 10.3 us -> 0 us
  other arithmetic: 10.2 us -> 0 us
    pallas_call x1, Pallas kernels: 188 us -> 156 us  [on_device(): pl.pallas_call(functools.partial(layer_kernel, nbits), out_shape=[jax.Sha...]
    pallas_call x0 -> x1, Pallas kernels: none -> 10.8 us  [on_device(): pl.pallas_call(finish_kernel, out_shape=[jax.ShapeDtypeStruct((L, 2304),...]
    convert_element_type x4 -> x0, other arithmetic: 10.2 us -> none  [the longest x1 4.57 us: on_device(): gu.astype(F32)]
    unnamed x16 -> x0, local copies, waits for them, and re-layouts: 6.09 us -> none
    slice x2 -> x0, local copies, waits for them, and re-layouts: 2.18 us -> none  [the longest x1 1.47 us: on_device(): fin[3]]
where the time goes in v2:
time: 167 us
  Pallas kernels  166 us (99%)
    pallas_call x1, Pallas kernels, on_device(): pl.pallas_call(functools.partial(layer_kernel, nbits), out_shape=[jax.Sha...  156 us
    pallas_call x1, Pallas kernels, on_device(): pl.pallas_call(finish_kernel, out_shape=[jax.ShapeDtypeStruct((L, 2304),...  10.8 us

profile of v2, /device:TPU:1, one launch (start us, length us, event | category | flops | bytes accessed | tf_op | source)
XLA Modules:
  0.0 167.2 jit_solution(7925415840342230966)
XLA Ops:
  0.6 155.5 %layer.1 = (bf16[1,768,768]{2,1,0:T(8,128)(2,1)}, f32[1,384,768]{2,1,0:T(8,128)}, f32[8,384]{1,0:T(8,128)}, bf16[2,384,3072]{2,1,0:T(8,128)(2,1)}, bf16[2,768,768]{2,1,0:T(8,128)(2,1)}) custom-call(bf16[1,384,768]{2,1,0:T(8,128)(2,1)} %clean_h.1, s32[1,384]{1,0:T(1,128)} %noise.1, bf16[384]{0:T(512)(128)(2,1)} %v_mask.1, bf16[384]{0:T(512)(128)(2,1)} %v_ga.1, ...), custom_call_target="tpu_custom_call" | custom-call | tf_op jit(solution)/shard_map/layer/pallas_call | solution.py:1192
  156.2 10.8 %finish.1 = (f32[384,2304]{1,0:T(8,128)}, f32[384,768]{1,0:T(8,128)}, f32[384,3072]{1,0:T(8,128)}, f32[1536,768]{1,0:T(8,128)}, bf16[1,768,768]{2,1,0:T(8,128)(2...) custom-call(bf16[2,384,3072]{2,1,0:T(8,128)(2,1)} %get-tuple-element, ...), custom_call_target="tpu_custom_call" | custom-call | tf_op jit(solution)/shard_map/finish/pallas_call | solution.py:1218

commit v3 on v2

--- a/solution.py
+++ b/solution.py
@@ -18,147 +18,151 @@
 F32 = jnp.float32
 MESH = pl.DeviceIdType.MESH
 LOGIT_SCALE = 0.125 * math.log2(math.e)
-N_SEND, N_RECV, N_LOCAL = 97, 190, 38
+N_SEND, N_RECV, N_LOCAL = 102, 182, 38
 NN = (((1,), (0,)), ((), ()))
 NT = (((1,), (1,)), ((), ()))
 TN = (((0,), (0,)), ((), ()))
 
 
 ROUTES = {
-    "d0": "0yZ",
+    "d0": "y0Z",
     "d1": "y0Z",
-    "d2": "y0Z",
-    "u0": "0yZ",
-    "u1": "y0Z",
-    "u2": "y012",
+    "d2": "y012",
+    "u0": "10y2",
+    "u1": "0y12",
+    "u2": "y0Z",
     "u3": "y012",
-    "u4": "y102",
-    "u5": "y012",
+    "u4": "1y02",
+    "u5": "1y02",
     "q0": "0y12",
-    "q1": "0yZ",
+    "q1": "y102",
     "q2": "y0Z",
-    "o": "y102",
+    "o": "0y12",
 }
 SCHEDULE = {
-    ("u", 0): (
+    ("b", 1): (
+        ("d0", 0),
+    ),
+    ("dn", 0): (
         ("d1", 0),
-    ),
-    ("u", 1): (
-        ("d0", 0),
-    ),
-    ("dn", 0): (
+        ("d0", 1),
+    ),
+    ("dn", 1): (
+        ("u0", 0),
+        ("u1", 0),
+    ),
+    ("dm", 0): (
+        ("u4", 0),
         ("d2", 0),
-        ("u0", 0),
-    ),
-    ("dn", 1): (
-        ("u1", 0),
         ("d1", 1),
     ),
-    ("dm", 0): (
+    ("att", 0): (
+        ("u0", 1),
+        ("u5", 0),
         ("u2", 0),
+    ),
+    ("att", 1): (
+        ("d0", 2),
+    ),
+    ("q", 0): (
+        ("u3", 0),
+        ("d1", 2),
+    ),
+    ("att", 2): (
+        ("o", 0),
+        ("u1", 1),
+    ),
+    ("att", 3): (
+        ("u4", 1),
+        ("u0", 2),
+        ("d0", 3),
         ("d2", 1),
     ),
-    ("att", 0): (
-        ("u1", 1),
-        ("d1", 2),
-        ("u3", 0),
-    ),
-    ("att", 1): (
+    ("q", 1): (
+        ("u5", 1),
         ("u2", 1),
+        ("u1", 2),
+    ),
+    ("att", 4): (
+        ("d1", 3),
+        ("o", 1),
+        ("u0", 3),
         ("d2", 2),
-        ("u4", 0),
-    ),
-    ("q", 0): (
+    ),
+    ("att", 5): (
+        ("u2", 2),
+        ("q0", 0),
+        ("u1", 3),
+    ),
+    ("q", 2): (
+        ("o", 2),
         ("u3", 1),
-        ("u1", 2),
-    ),
-    ("att", 2): (
-        ("u2", 2),
-        ("u5", 0),
-    ),
-    ("att", 3): (
-        ("d1", 3),
-        ("d0", 1),
-    ),
-    ("q", 1): (
-        ("u4", 1),
-        ("d2", 3),
-        ("q0", 0),
-        ("u3", 2),
-        ("u0", 1),
-    ),
-    ("att", 4): (
-        ("u1", 3),
-        ("u5", 1),
-        ("u2", 3),
-    ),
-    ("att", 5): (
-        ("d1", 4),
-        ("o", 0),
-        ("d0", 2),
-        ("u3", 3),
-        ("u5", 2),
-    ),
-    ("q", 2): (
-        ("q0", 1),
-        ("u0", 2),
-    ),
-    ("da", 0): (
-        ("u2", 4),
+        ("u0", 4),
         ("q1", 0),
         ("u4", 2),
-        ("o", 1),
+        ("d2", 3),
+    ),
+    ("da", 0): (
+        ("u2", 3),
+        ("q0", 1),
     ),
     ("da", 1): (
-        ("d0", 3),
-        ("u3", 4),
+        ("u1", 4),
+        ("u3", 2),
+        ("d0", 4),
+        ("o", 3),
+        ("u5", 2),
+        ("q1", 1),
+        ("u4", 3),
+    ),
+    ("bo", 0): (
         ("d2", 4),
-        ("u5", 3),
-    ),
-    ("bo", 0): (
+        ("s", 0),
+        ("d1", 4),
         ("q2", 0),
         ("q0", 2),
-        ("u1", 4),
-        ("u0", 3),
-        ("o", 2),
-        ("q1", 1),
-        ("u2", 5),
+        ("u0", 5),
+        ("u1", 5),
+        ("u3", 3),
     ),
     ("bo", 1): (
-        ("s", 0),
-        ("u4", 3),
+        ("u2", 4),
+        ("o", 4),
+        ("u5", 3),
+        ("q1", 2),
+        ("s", 1),
+        ("u4", 4),
+        ("d2", 5),
+    ),
+    "tail": (
+        ("q0", 3),
+        ("q2", 1),
+        ("u0", 6),
+        ("u3", 4),
+        ("u1", 6),
+        ("s", 2),
+        ("o", 5),
+        ("u4", 5),
+        ("u5", 4),
+        ("q1", 3),
+        ("q0", 4),
+        ("d2", 6),
+        ("q2", 2),
         ("u3", 5),
-        ("u5", 4),
-        ("q0", 3),
-        ("d0", 4),
-    ),
-    "tail": (
-        ("o", 3),
-        ("q2", 1),
+        ("s", 3),
+        ("o", 6),
+        ("u4", 6),
         ("u5", 5),
-        ("q1", 2),
-        ("u0", 4),
-        ("u4", 4),
-        ("q0", 4),
-        ("u2", 6),
-        ("s", 1),
-        ("o", 4),
+        ("q1", 4),
+        ("q0", 5),
         ("u3", 6),
+        ("q1", 5),
+        ("q2", 3),
+        ("s", 4),
         ("u5", 6),
-        ("q2", 2),
-        ("q0", 5),
-        ("u4", 5),
-        ("o", 5),
-        ("q1", 3),
-        ("s", 2),
         ("q0", 6),
-        ("q2", 3),
-        ("u4", 6),
-        ("q1", 4),
-        ("o", 6),
-        ("s", 3),
+        ("q1", 6),
         ("q2", 4),
-        ("s", 4),
     ),
 }
 
@@ -190,9 +194,9 @@
     nbits,
     clean_h, noise, v_mask, v_ga, v_gm, v_bd, v_bu, cos_r, sin_r, wq_h, wo_h, wu_h, wd_h, og_h,
     out_h, cg_h, fin, o1_h, od_h,
-    small_in, small, prow, mcol, mbf, mbb, mbe,
+    small_in, small, prow, mcol, mbb, mbe,
     stream, normed, wq, wo, wu, wd, og,
-    qkv, qaug, mixed, aa, nm, act, dpre, xs, xr, daf, db, dm, dks, dsn,
+    qkv, lbuf, mixed, aa, nm, act, dpre, xs, xr, daf, db, dm, dks,
     gd, g1, r0d, r01, r1d, r11, r2d, r21, r3d, r31, red, re1,
     sbuf, srec, ss, rs, ls,
 ):
@@ -324,31 +328,62 @@
 
     xw_q = spread_q(peers[0])
     zw_q = spread_q(peers[1])
-    yw_u = remote(
-        lambda k, h: rc(
+    def half_of(i):
+        if isinstance(i, int):
+            return 1 - f if i == 0 else f
+        return (1 - f) * (1 - i) + f * i
+
+    def up_lanes(i):
+        return pl.ds(mo(half_of(i) * D, 128), D)
+
+    def y_wu_to(unit):
+        rows = mo(96 * unit, 16)
+
+        def make(k, i):
+            h = f if i == 0 else 1 - f
+            return rc(
+                k,
+                wu_h.at[pl.ds(rows, 96), pl.ds(mo(h * 1536 + c * D, 128), D)],
+                wu.at[pl.ds(mo(f * L + rows, 16), 96), pl.ds(mo(h * D, 128), D)],
+                ypeer,
+            )
+
+        return remote(make, 2)
+
+    def spread_u(dev):
+        rows = mo(other + 96 * u, 16)
+        return remote(
+            lambda k, i: rc(
+                k, wu.at[pl.ds(rows, 96), up_lanes(i)], wu.at[pl.ds(rows, 96), up_lanes(i)], dev
+            ),
+            2,
+        )
+
+    yw_u = y_wu_to(u)
+    yw_u2 = y_wu_to(3 - u)
+    xw_u = spread_u(peers[0])
+    zw_u = spread_u(peers[1])
+    ux, uz = 2 * bits[1] + 1 - bits[0], 2 * (1 - bits[1]) + bits[0]
+    odown = mo((1 - f) * D, 128)
+    yw_d = remote(
+        lambda k, i: rc(
             k,
-            wu_h.at[pl.ds(mo(96 * u, 16), 96), pl.ds(mo(h * 1536 + c * D, 128), D)],
-            wu.at[pl.ds(mo(f * L + 96 * u, 16), 96), pl.ds(h * D, D)],
+            wd_h.at[pl.ds(mo(c * D + 192 * u + 96 * i, 16), 96)],
+            wd.at[pl.ds(mo(f * D + 192 * u + 96 * i, 16), 96)],
             ypeer,
         ),
         2,
     )
-    ux, uz = 2 * bits[1] + 1 - bits[0], 2 * (1 - bits[1]) + bits[0]
-    xw_u = spread(wu, other, 96, u, peers[0])
-    zw_u = spread(wu, other, 96, u, peers[1])
-    xw_u2 = spread(wu, other, 48, 2 * uz, peers[0])
-    zw_u2 = spread(wu, other, 48, 2 * ux + 1, peers[1])
-    odown = mo((1 - f) * D, 128)
-    yw_d = remote(
-        lambda k, i: rc(
-            k,
-            wd_h.at[pl.ds(mo(c * D + 192 * u, 16), 192)],
-            wd.at[pl.ds(mo(f * D + 192 * u, 16), 192)],
-            ypeer,
-        )
-    )
-    xw_d = spread(wd, odown, 192, u, peers[0])
-    zw_d = spread(wd, odown, 192, u, peers[1])
+
+    def spread_d(dev):
+        def make(k, i):
+            rows = pl.ds(mo(odown + 192 * u + 96 * i, 16), 96)
+            return rc(k, wd.at[rows], wd.at[rows], dev)
+
+        return remote(make, 2)
+
+    xw_d = spread_d(peers[0])
+    zw_d = spread_d(peers[1])
     xw_d2 = spread(wd, odown, 96, 2 * uz, peers[0])
     zw_d2 = spread(wd, odown, 96, 2 * ux + 1, peers[1])
     yw_o = remote(
@@ -585,10 +620,12 @@
         yw_q(j).start()
     for j in range(3):
         yw_q2(j).start()
-    for h in range(2):
-        yw_u(h).start()
     yw_o().start()
-    yw_d().start()
+    for i in range(2):
+        yw_u(i).start()
+        yw_u2(i).start()
+    for i in range(2):
+        yw_d(i).start()
     for cp in l_og + l_wu + [l_wo, l_wd]:
         cp().start()
 
@@ -596,13 +633,9 @@
     low_half = lane < HD
     rot_low = lax.rem(lane, HD) < HD // 2
     bm = [jnp.where(low_half, 1.0, 0.0).astype(BF), jnp.where(low_half, 0.0, 1.0).astype(BF)]
-    selm = [low_half, lane >= HD]
-    spare = [HD, 0]
     ir = lax.div(lax.broadcasted_iota(jnp.int32, (128, 128), 0), BLOCK)
     ic = lax.div(lax.broadcasted_iota(jnp.int32, (128, 128), 1), BLOCK)
     neg = -1e30
-    mbf[0:128, :] = jnp.where(ic < ir, 0.0, neg)
-    mbf[128:256, :] = jnp.where(ic <= ir, 0.0, neg)
     mbb[:, 0:128] = jnp.where(ir < ic, 0.0, neg)
     mbb[:, 128:256] = jnp.where(ir <= ic, 0.0, neg)
     mbe[...] = jnp.where(ir == ic, 0.0, neg)
@@ -674,11 +707,6 @@
         return carry
 
     lax.fori_loop(0, 2 * NT3, qkv_rows, 0)
-    for h in range(2):
-        l_wu[h]().wait()
-        yw_u(h).wait_recv()
-    xw_u().start()
-    zw_u().start()
 
     def run_at(idx, table):
         for k, fns in table.items():
@@ -692,29 +720,26 @@
         yw_o().wait_recv()
         xw_o().start()
 
-    def w_u_2():
-        xw_u().wait_recv()
-        zw_u().wait_recv()
-        xw_u2().start()
-        zw_u2().start()
-
     def w_o_2():
         xw_o().wait_recv()
         sw_o().start()
 
-    def w_d_1():
-        l_wd().wait()
-        yw_d().wait_recv()
-        xw_d().start()
-        zw_d().start()
-
-    def w_d_2():
-        xw_d().wait_recv()
-        zw_d().wait_recv()
-        xw_d2().start()
-        zw_d2().start()
-
-    fwd_events = {2: [w_o_1], 3: [w_u_2, w_o_2], 4: [w_d_1]}
+    def w_u(i):
+        yw_u(i).wait_recv()
+        xw_u(i).start()
+        zw_u(i).start()
+
+    def w_u_end(i):
+        yw_u2(i).wait_recv()
+        xw_u(i).wait_recv()
+        zw_u(i).wait_recv()
+
+    def w_d(i):
+        yw_d(i).wait_recv()
+        xw_d(i).start()
+        zw_d(i).start()
+
+    fwd_events = {0: [w_o_1], 2: [lambda: w_u(0)], 4: [w_o_2]}
 
     def attn_fwd(n, carry):
         s, p = 1 - lax.div(n, 3), lax.rem(n, 3)
@@ -726,44 +751,40 @@
         def rws(a, m):
             return pl.ds(mo(r0 + a, 128), m)
 
+        kcl = [qkv[rws(256 * j + 128, 128), lk] for j in range(NT3)]
+        vcl = [qkv[rws(256 * j + 128, 128), lv] for j in range(NT3)]
+        blocks = [(i, a) for i in range(NT3) for a in range(2)]
+        sc, pr, mixes = {}, {}, {}
+        for i, a in blocks:
+            q = qkv[rws(256 * i, 256), lq]
+            kc = jnp.concatenate(kcl[: i + 1], axis=0) * bm[a]
+            st = dot(kc, q, NT) * LOGIT_SCALE
+            kn = qkv[rws(256 * i, 128), lk] * bm[a]
+            sn = dot(kn, q[:128], NT) * LOGIT_SCALE + mbe[...]
+            last = st[128 * i :] + mbb[...]
+            st = last if i == 0 else jnp.concatenate([st[: 128 * i], last], axis=0)
+            sc[i, a] = st, sn
+        for i, a in blocks:
+            st, sn = sc[i, a]
+            m1 = jnp.max(st, axis=0, keepdims=True)
+            mn = jnp.maximum(m1[:, :128], jnp.max(sn, axis=0, keepdims=True))
+            m = jnp.concatenate([mn, m1[:, 128:]], axis=1)
+            pt, pn = jnp.exp2(st - m), jnp.exp2(sn - mn)
+            tot = jnp.sum(pt, axis=0, keepdims=True)
+            totn = tot[:, :128] + jnp.sum(pn, axis=0, keepdims=True)
+            tot = jnp.concatenate([totn, tot[:, 128:]], axis=1)
+            lbuf[(s * 3 + p) * 2 + a, :, 256 * i : 256 * i + 256] = m + jnp.log2(tot)
+            pr[i, a] = pt.astype(BF), pn.astype(BF)
+        for i, a in blocks:
+            vc = jnp.concatenate(vcl[: i + 1], axis=0) * bm[a] + bm[1 - a]
+            vn = qkv[rws(256 * i, 128), lv] * bm[a] + bm[1 - a]
+            o = dot(pr[i, a][0], vc, TN)
+            mixes[i, a] = jnp.concatenate([o[:128] + dot(pr[i, a][1], vn, TN), o[128:]], axis=0)
         for i in range(NT3):
-            res = []
-            for a in range(2):
-                q = qkv[rws(256 * i, 256), lq] * bm[a]
-                kc = jnp.concatenate(
-                    [qkv[rws(256 * j + 128, 128), lk] for j in range(i + 1)], axis=0
-                )
-                vc = jnp.concatenate(
-                    [qkv[rws(256 * j + 128, 128), lv] for j in range(i + 1)], axis=0
-                ) * bm[a] + bm[1 - a]
-                vn = qkv[rws(256 * i, 128), lv] * bm[a] + bm[1 - a]
-                s1 = dot(q, kc, NT) * LOGIT_SCALE
-                sn = dot(q[:128], qkv[rws(256 * i, 128), lk], NT) * LOGIT_SCALE + mbe[...]
-                last = s1[:, 128 * i :] + mbf[...]
-                s1 = last if i == 0 else jnp.concatenate([s1[:, : 128 * i], last], axis=1)
-                m1 = jnp.max(s1, axis=1, keepdims=True)
-                mn = jnp.maximum(m1[:128], jnp.max(sn, axis=1, keepdims=True))
-                m = jnp.concatenate([mn, m1[128:]], axis=0)
-                p1 = jnp.exp2(s1 - m).astype(BF)
-                pn = jnp.exp2(sn - mn).astype(BF)
-                o = dot(p1, vc)
-                o = jnp.concatenate([o[:128] + dot(pn, vn), o[128:]], axis=0)
-                val = (m + jnp.log2(o)) * (-1.0 / LOGIT_SCALE)
-                hi = val.astype(BF).astype(F32)
-                mid = (val - hi).astype(BF).astype(F32)
-                lo = val - hi - mid
-                extra = jnp.where(
-                    lane == spare[a], hi,
-                    jnp.where(lane == spare[a] + 1, mid, jnp.where(lane == spare[a] + 2, lo, 0.0)),
-                )
-                qaug[rws(256 * i, 256), pl.ds(mo(256 * p + 128 * a, 128), 128)] = jnp.where(
-                    selm[a], q.astype(F32), extra
-                ).astype(BF)
-                res.append(o)
-            data = jnp.where(low_half, res[0], res[1])
-            sums = pltpu.roll(jnp.where(low_half, res[1], res[0]), HD, 1)
+            o0, o1 = mixes[i, 0], mixes[i, 1]
+            sums = pltpu.roll(jnp.where(low_half, o1, o0), HD, 1)
             mixed[rws(256 * i, 256), pl.ds(mo(c * L + 128 * p, 128), 128)] = (
-                data * (1.0 / sums)
+                jnp.where(low_half, o0, o1) * (1.0 / sums)
             ).astype(BF)
         s_mix(n).start()
         run_at(n, fwd_events)
@@ -784,12 +805,17 @@
         return carry
 
     lax.fori_loop(0, NT3, out_proj, 0)
-    xw_u2().wait_recv()
-    zw_u2().wait_recv()
+    for h in range(2):
+        l_wu[h]().wait()
+    w_u_end(0)
+    w_u(1)
 
     for n in range(2):
-        h = 1 - f if n == 0 else f
-        lanes = pl.ds(mo(h * D, 128), D)
+        h = half_of(n)
+        lanes = up_lanes(n)
+        if n == 1:
+            w_u_end(1)
+            w_d(0)
         bu = jnp.concatenate(
             [small[h, pl.ds(4 + 2 * c + r, 1), :] for r in range(2)], axis=1
         )
@@ -816,7 +842,8 @@
         lax.fori_loop(0, 4, rows_a, 0)
         if n == 0:
             s_og().wait_recv()
-            w_d_2()
+        else:
+            w_d(1)
 
         def down_grad(k, carry, n=n, h=h):
             at = mo(h * D + 256 * k, 128)
@@ -830,11 +857,13 @@
 
         handle(("a", n))
         lax.fori_loop(0, 3, down_grad, 0)
-    xw_d2().wait_recv()
-    zw_d2().wait_recv()
+    zw_d(0).wait_recv()
+    xw_d2().start()
+    l_wd().wait()
 
     for n in range(2):
-        lanes = pl.ds(n * D, D)
+        h = half_of(1 - n)
+        lanes = up_lanes(1 - n)
 
         def rows_b(r, tot, lanes=lanes):
             rows = pl.ds(mo(L * r, 128), L)
@@ -842,8 +871,17 @@
             dpre[rows, lanes] = g.astype(BF)
             return tot + jnp.sum(g, axis=0, keepdims=True)
 
-        sbuf[0, 4 + n : 5 + n, :] = lax.fori_loop(0, 4, rows_b, jnp.zeros((1, D), F32))
+        if n == 1:
+            xw_d(0).wait_recv()
+            zw_d(1).wait_recv()
+            xw_d2().wait_recv()
+            zw_d2().wait_recv()
+        sbuf[0, pl.ds(4 + h, 1), :] = lax.fori_loop(0, 4, rows_b, jnp.zeros((1, D), F32))
+        if n == 0:
+            xw_d(1).wait_recv()
+            zw_d2().start()
         handle(("b", n))
+    for n in range(2):
         g1[:, n * D : n * D + D] = dot(nm[...], dpre[:, n * D : n * D + D], TN).astype(BF)
         for t in range(3 * n, 3 * n + 3):
             chunks[f"u{t}"].start()
@@ -891,12 +929,9 @@
     chunks["o"].start()
     handle(("dm", 0))
 
-    one_q = [
-        jnp.where((lane >= s) & (lane < s + 3), 1.0, 0.0).astype(BF) for s in spare
-    ]
-    one_d = [
-        jnp.where((lane >= s) & (lane < s + 2), 1.0, 0.0).astype(BF) for s in spare
-    ]
+    pick_lane = lax.rem(lax.broadcasted_iota(jnp.int32, (8, 256), 1), 128)
+    pick_row = lax.broadcasted_iota(jnp.int32, (8, 256), 0)
+    pick = jnp.where(pick_row == lax.div(pick_lane, HD), 1.0, 0.0).astype(BF)
 
     def attn_bwd(n, carry):
         s, p = lax.rem(n, 2), lax.div(n, 2)
@@ -908,67 +943,73 @@
         def rws(a, m):
             return pl.ds(mo(r0 + a, 128), m)
 
-        dog = dm[rws(0, T), lq]
-        prod = dog.astype(F32) * mixed[
+        prod = dm[rws(0, T), lq].astype(F32) * mixed[
             rws(0, T), pl.ds(mo(c * L + 128 * p, 128), 128)
         ].astype(F32)
-        doa = []
-        for a in range(2):
-            val = -jnp.sum(jnp.where(selm[a], prod, 0.0), axis=1, keepdims=True)
-            hi = val.astype(BF).astype(F32)
-            mid = val - hi
-            extra = jnp.where(lane == spare[a], hi, jnp.where(lane == spare[a] + 1, mid, 0.0))
-            doa.append(jnp.where(selm[a], dog.astype(F32), extra).astype(BF))
+        hi = prod.astype(BF)
+        lo = (prod - hi.astype(F32)).astype(BF)
+        drow = dot(pick, jnp.concatenate([hi, lo], axis=1), NT)
+
+        def heads(x, y):
+            return jnp.where(low_half, x, y)
+
+        blocks = [(kt, a) for kt in range(NT3) for a in range(2)]
+        sc, dp, res = {}, {}, {}
+        for kt, a in blocks:
+            q0, nq = 256 * kt, T - 256 * kt
+            q = qkv[rws(q0, nq), lq]
+            lt = lbuf[(s * 3 + p) * 2 + a][:, q0:]
+            kc = qkv[rws(q0 + 128, 128), lk] * bm[a]
+            kn = qkv[rws(q0, 128), lk] * bm[a]
+            st = dot(kc, q, NT) * LOGIT_SCALE - lt
+            first = st[:, :256] + mbb[...]
+            st = first if nq == 256 else jnp.concatenate([first, st[:, 256:]], axis=1)
+            sn = dot(kn, q[:128], NT) * LOGIT_SCALE - lt[:, :128] + mbe[...]
+            sc[kt, a] = st, sn
+        for kt, a in blocks:
+            q0, nq = 256 * kt, T - 256 * kt
+            do = dm[rws(q0, nq), lq]
+            vc = qkv[rws(q0 + 128, 128), lv] * bm[a]
+            vn = qkv[rws(q0, 128), lv] * bm[a]
+            dr = drow[a : a + 1, q0:]
+            dp[kt, a] = dot(vc, do, NT) - dr, dot(vn, do[:128], NT) - dr[:, :128]
+        for b in blocks:
+            pt, pn = jnp.exp2(sc[b][0]), jnp.exp2(sc[b][1])
+            res[b] = (
+                (pt * dp[b][0]).astype(BF), (pn * dp[b][1]).astype(BF),
+                pt.astype(BF), pn.astype(BF),
+            )
         for kt in range(NT3):
-            q0 = 256 * kt
-            nq = T - q0
-            pts, dss, ptn, dsnn = [], [], [], []
+            q0, nq = 256 * kt, T - 256 * kt
+            q, do = qkv[rws(q0, nq), lq], dm[rws(q0, nq), lq]
+            r0_, r1_ = res[kt, 0], res[kt, 1]
+            dks[pl.ds(q0 + 128, 128), :] = heads(dot(r0_[0], q), dot(r1_[0], q))
+            dks[pl.ds(q0, 128), :] = heads(dot(r0_[1], q[:128]), dot(r1_[1], q[:128]))
+            qkv[rws(q0 + 128, 128), lv] = heads(dot(r0_[2], do), dot(r1_[2], do)).astype(BF)
+            qkv[rws(q0, 128), lv] = heads(
+                dot(r0_[3], do[:128]), dot(r1_[3], do[:128])
+            ).astype(BF)
+        dqs = []
+        for i in range(NT3):
+            kc = jnp.concatenate([qkv[rws(256 * j + 128, 128), lk] for j in range(i + 1)], axis=0)
+            kn = qkv[rws(256 * i, 128), lk]
+            both = []
             for a in range(2):
-                qa = qaug[rws(q0, nq), pl.ds(mo(256 * p + 128 * a, 128), 128)]
-                da = doa[a][q0:]
-                kc = qkv[rws(q0 + 128, 128), lk] * bm[a] + one_q[a]
-                kn = qkv[rws(q0, 128), lk] * bm[a] + one_q[a]
-                vc = qkv[rws(q0 + 128, 128), lv] * bm[a] + one_d[a]
-                vn = qkv[rws(q0, 128), lv] * bm[a] + one_d[a]
-                st = dot(kc, qa, NT) * LOGIT_SCALE
-                first = st[:, :256] + mbb[...]
-                st = first if nq == 256 else jnp.concatenate([first, st[:, 256:]], axis=1)
-                pt = jnp.exp2(st)
-                ds = pt * dot(vc, da, NT)
-                dpre[pl.ds(512 * a + 128 * kt, 128), pl.ds(q0, nq)] = ds.astype(BF)
-                pts.append(pt.astype(BF))
-                dss.append(ds.astype(BF))
-                pn = jnp.exp2(dot(kn, qa[:128], NT) * LOGIT_SCALE + mbe[...])
-                dn = pn * dot(vn, da[:128], NT)
-                dsn[a, kt] = dn.astype(BF)
-                ptn.append(pn.astype(BF))
-                dsnn.append(dn.astype(BF))
-            dom = [dm[rws(q0, nq), lq] * bm[a] for a in range(2)]
-            qm = [qkv[rws(q0, nq), lq] * bm[a] for a in range(2)]
-            domc, qmc = jnp.concatenate(dom, axis=0), jnp.concatenate(qm, axis=0)
-            domn = jnp.concatenate([x[:128] for x in dom], axis=0)
-            qmn = jnp.concatenate([x[:128] for x in qm], axis=0)
-            dks[pl.ds(q0 + 128, 128), :] = dot(jnp.concatenate(dss, axis=1), qmc)
-            dks[pl.ds(q0, 128), :] = dot(jnp.concatenate(dsnn, axis=1), qmn)
-            qkv[rws(q0 + 128, 128), lv] = dot(jnp.concatenate(pts, axis=1), domc).astype(BF)
-            qkv[rws(q0, 128), lv] = dot(jnp.concatenate(ptn, axis=1), domn).astype(BF)
-        for i in range(NT3):
-            dq = None
-            for a in range(2):
-                kc = jnp.concatenate(
-                    [qkv[rws(256 * j + 128, 128), lk] for j in range(i + 1)], axis=0
-                ) * bm[a]
-                part = dot(
-                    dpre[pl.ds(512 * a, 128 * (i + 1)), pl.ds(256 * i, 256)], kc, TN
+                ds = jnp.concatenate(
+                    [
+                        res[kt, a][0][:, 256 * (i - kt) : 256 * (i - kt) + 256]
+                        for kt in range(i + 1)
+                    ],
+                    axis=0,
                 )
-                pn = dot(dsn[a, i], qkv[rws(256 * i, 128), lk] * bm[a], TN)
-                part = jnp.concatenate([part[:128] + pn, part[128:]], axis=0)
-                dq = part if dq is None else dq + part
-            cos, sin = rows2(cos_r, i), rows2(sin_r, i)
-            qkv[rws(256 * i, 256), lq] = (turn(dq, cos, -sin) * 0.125).astype(BF)
+                x = dot(ds, kc, TN)
+                x = jnp.concatenate([x[:128] + dot(res[i, a][1], kn, TN), x[128:]], axis=0)
+                both.append(x)
+            dqs.append(heads(*both))
         for i in range(NT3):
             cos, sin = rows2(cos_r, i), rows2(sin_r, i)
             dk = dks[pl.ds(256 * i, 256), :]
+            qkv[rws(256 * i, 256), lq] = (turn(dqs[i], cos, -sin) * 0.125).astype(BF)
             qkv[rws(256 * i, 256), lk] = (turn(dk, cos, -sin) * 0.125).astype(BF)
         handle_at(n, {i: ("att", i) for i in range(6)})
 
@@ -1174,14 +1215,13 @@
     hbm = pl.BlockSpec(memory_space=pltpu.HBM)
     vm = pl.BlockSpec(memory_space=pltpu.VMEM)
     scratch = [
-        ((8, L), F32), ((2, 8, L), F32), ((8, D), F32), ((L, 128), F32), ((256, 128), F32),
+        ((8, L), F32), ((2, 8, L), F32), ((8, D), F32), ((L, 128), F32),
         ((128, 256), F32), ((128, 128), F32),
         ((T, D), BF), ((2 * T, D), BF), ((D, 1152), BF), ((D, D), BF), ((D, 1536), BF),
         ((1536, D), BF), ((2 * T, D), BF),
-        ((2 * T, 1152), BF), ((2 * T, D), BF), ((2 * T, D), BF), ((T, D), F32),
+        ((2 * T, 1152), BF), ((12, 1, T), F32), ((2 * T, D), BF), ((T, D), F32),
         ((2 * T, D), BF), ((2 * T, 1536), BF), ((2 * T, 1536), BF), ((T, D), BF),
         ((T, D), BF), ((T, D), F32), ((2 * T, D), BF), ((2 * T, L), BF), ((T, 128), F32),
-        ((2, 3, 128, 128), BF),
         ((1536, D), BF), ((D, 3072), BF),
         ((D, D), BF), ((L, 3072), BF), ((L, D), BF), ((192, 3072), BF),
         ((192, D), BF), ((96, 3072), BF), ((96, D), BF), ((48, 3072), BF),
@@ -1202,8 +1242,8 @@
         out_specs=[hbm, hbm, vm, hbm, hbm],
         scratch_shapes=[pltpu.VMEM(s, t) for s, t in scratch]
         + [
-            pltpu.SemaphoreType.DMA((N_SEND,)),
-            pltpu.SemaphoreType.DMA((N_RECV + 20 * (nx - 1),)),
+            pltpu.SemaphoreType.DMA((N_SEND + 1 * (nbits - 3),)),
+            pltpu.SemaphoreType.DMA((N_RECV + 14 * (nbits - 3),)),
             pltpu.SemaphoreType.DMA((N_LOCAL,)),
         ],
         compiler_params=pltpu.CompilerParams(

time: 167 us -> 156 us (0.934)
  Pallas kernels: 166 us -> 155 us
    pallas_call x1, Pallas kernels: 156 us -> 144 us  [on_device(): pl.pallas_call(functools.partial(layer_kernel, nbits), out_shape=[jax.Sha...]
where the time goes in v3:
time: 156 us
  Pallas kernels  155 us (99%)
    pallas_call x1, Pallas kernels, on_device(): pl.pallas_call(functools.partial(layer_kernel, nbits), out_shape=[jax.Sha...  144 us
    pallas_call x1, Pallas kernels, on_device(): pl.pallas_call(finish_kernel, out_shape=[jax.ShapeDtypeStruct((L, 2304),...  10.8 us

profile of v3, /device:TPU:1, one launch (start us, length us, event | category | flops | bytes accessed | tf_op | source)
XLA Modules:
  0.0 155.9 jit_solution(17004945978867576949)
XLA Ops:
  0.6 144.3 %layer.1 = (bf16[1,768,768]{2,1,0:T(8,128)(2,1)}, f32[1,384,768]{2,1,0:T(8,128)}, f32[8,384]{1,0:T(8,128)}, bf16[2,384,3072]{2,1,0:T(8,128)(2,1)}, bf16[2,768,768]{2,1,0:T(8,128)(2,1)}) custom-call(bf16[1,384,768]{2,1,0:T(8,128)(2,1)} %clean_h.1, s32[1,384]{1,0:T(1,128)} %noise.1, bf16[384]{0:T(512)(128)(2,1)} %v_mask.1, bf16[384]{0:T(512)(128)(2,1)} %v_ga.1, ...), custom_call_target="tpu_custom_call" | custom-call | tf_op jit(solution)/shard_map/layer/pallas_call | solution.py:1232
  144.9 10.8 %finish.1 = (f32[384,2304]{1,0:T(8,128)}, f32[384,768]{1,0:T(8,128)}, f32[384,3072]{1,0:T(8,128)}, f32[1536,768]{1,0:T(8,128)}, bf16[1,768,768]{2,1,0:T(8,128)(2...) custom-call(bf16[2,384,3072]{2,1,0:T(8,128)(2,1)} %get-tuple-element, ...), custom_call_target="tpu_custom_call" | custom-call | tf_op jit(solution)/shard_map/finish/pallas_call | solution.py:1258

commit v4 on v3

--- a/solution.py
+++ b/solution.py
@@ -18,7 +18,7 @@
 F32 = jnp.float32
 MESH = pl.DeviceIdType.MESH
 LOGIT_SCALE = 0.125 * math.log2(math.e)
-N_SEND, N_RECV, N_LOCAL = 102, 182, 38
+N_SEND, N_RECV, N_LOCAL = 102, 185, 38
 NN = (((1,), (0,)), ((), ()))
 NT = (((1,), (1,)), ((), ()))
 TN = (((0,), (0,)), ((), ()))
@@ -26,14 +26,14 @@
 
 ROUTES = {
     "d0": "y0Z",
-    "d1": "y0Z",
-    "d2": "y012",
-    "u0": "10y2",
-    "u1": "0y12",
-    "u2": "y0Z",
-    "u3": "y012",
-    "u4": "1y02",
-    "u5": "1y02",
+    "d1": "0y12",
+    "d2": "y0Z",
+    "u0": "y012",
+    "u1": "y0Z",
+    "u2": "10y2",
+    "u3": "1y02",
+    "u4": "y0Z",
+    "u5": "y0Z",
     "q0": "0y12",
     "q1": "y102",
     "q2": "y0Z",
@@ -45,121 +45,115 @@
     ),
     ("dn", 0): (
         ("d1", 0),
+        ("d2", 0),
+    ),
+    ("dn", 1): (
+        ("u2", 0),
         ("d0", 1),
-    ),
-    ("dn", 1): (
         ("u0", 0),
+    ),
+    ("dm", 0): (
+        ("u3", 0),
+        ("d2", 1),
         ("u1", 0),
     ),
-    ("dm", 0): (
+    ("att", 0): (
+        ("u2", 1),
         ("u4", 0),
-        ("d2", 0),
-        ("d1", 1),
-    ),
-    ("att", 0): (
         ("u0", 1),
+        ("d0", 2),
+    ),
+    ("q", 0): (
         ("u5", 0),
-        ("u2", 0),
-    ),
-    ("att", 1): (
-        ("d0", 2),
-    ),
-    ("q", 0): (
-        ("u3", 0),
-        ("d1", 2),
+        ("u0", 2),
+        ("d2", 2),
     ),
     ("att", 2): (
         ("o", 0),
+        ("d1", 1),
         ("u1", 1),
     ),
     ("att", 3): (
+        ("d0", 3),
+        ("u0", 3),
+        ("u3", 1),
         ("u4", 1),
-        ("u0", 2),
-        ("d0", 3),
-        ("d2", 1),
+        ("u2", 2),
     ),
     ("q", 1): (
+        ("d1", 2),
+    ),
+    ("att", 4): (
+        ("d2", 3),
+        ("o", 1),
+        ("u1", 2),
+    ),
+    ("att", 5): (
+        ("q0", 0),
+        ("u0", 4),
         ("u5", 1),
-        ("u2", 1),
-        ("u1", 2),
-    ),
-    ("att", 4): (
-        ("d1", 3),
-        ("o", 1),
-        ("u0", 3),
-        ("d2", 2),
-    ),
-    ("att", 5): (
-        ("u2", 2),
-        ("q0", 0),
-        ("u1", 3),
+        ("u4", 2),
     ),
     ("q", 2): (
         ("o", 2),
-        ("u3", 1),
-        ("u0", 4),
+        ("u2", 3),
+    ),
+    ("da", 0): (
         ("q1", 0),
-        ("u4", 2),
-        ("d2", 3),
-    ),
-    ("da", 0): (
-        ("u2", 3),
+        ("d1", 3),
+        ("u0", 5),
+        ("d0", 4),
+        ("u3", 2),
+        ("u1", 3),
+    ),
+    ("da", 1): (
         ("q0", 1),
-    ),
-    ("da", 1): (
+        ("u5", 2),
+        ("d2", 4),
+        ("u4", 3),
+    ),
+    ("bo", 0): (
+        ("o", 3),
+        ("s", 0),
+        ("q1", 1),
+        ("u0", 6),
+        ("u2", 4),
+        ("q2", 0),
         ("u1", 4),
-        ("u3", 2),
-        ("d0", 4),
-        ("o", 3),
-        ("u5", 2),
-        ("q1", 1),
-        ("u4", 3),
-    ),
-    ("bo", 0): (
-        ("d2", 4),
-        ("s", 0),
         ("d1", 4),
-        ("q2", 0),
         ("q0", 2),
-        ("u0", 5),
-        ("u1", 5),
+    ),
+    ("bo", 1): (
         ("u3", 3),
-    ),
-    ("bo", 1): (
-        ("u2", 4),
-        ("o", 4),
+        ("u4", 4),
+        ("s", 1),
         ("u5", 3),
         ("q1", 2),
-        ("s", 1),
-        ("u4", 4),
-        ("d2", 5),
     ),
     "tail": (
+        ("u2", 5),
+        ("d1", 5),
+        ("o", 4),
         ("q0", 3),
+        ("u3", 4),
         ("q2", 1),
-        ("u0", 6),
-        ("u3", 4),
-        ("u1", 6),
         ("s", 2),
+        ("q1", 3),
+        ("u2", 6),
+        ("u5", 4),
         ("o", 5),
-        ("u4", 5),
-        ("u5", 4),
-        ("q1", 3),
         ("q0", 4),
-        ("d2", 6),
         ("q2", 2),
+        ("s", 3),
+        ("d1", 6),
+        ("q1", 4),
         ("u3", 5),
-        ("s", 3),
+        ("q0", 5),
         ("o", 6),
-        ("u4", 6),
-        ("u5", 5),
-        ("q1", 4),
-        ("q0", 5),
+        ("q2", 3),
+        ("q1", 5),
+        ("s", 4),
         ("u3", 6),
-        ("q1", 5),
-        ("q2", 3),
-        ("s", 4),
-        ("u5", 6),
         ("q0", 6),
         ("q1", 6),
         ("q2", 4),
@@ -453,16 +447,36 @@
             return g.at[pl.ds(mo(gbase(h) + off, 16), n), lanes]
 
         def rreg(stage, at, n):
-            return recv[stage].at[pl.ds((rbase >> stage) + at, n), lanes]
+            return recv[stage].at[pl.ds((rbase >> (0, 1, 1, 2)[stage]) + at, n), lanes]
 
         def oreg(core, off, n):
             return oref.at[core, pl.ds(mo(orow + off, 16), n), lanes]
 
-        def send(copies, before=()):
-            for cp in before:
-                cp().wait_send()
-            for cp in copies:
-                cp().start()
+        def at_role(role, fn):
+            if role is None:
+                fn()
+            else:
+                pl.when(role)(fn)
+
+        class Stage:
+            def __init__(self, copies, sums=(), sender=None, receiver=None):
+                self.copies, self.sums = copies, sums
+                self.sender, self.receiver = sender, receiver
+
+            def start(self):
+                at_role(self.sender, lambda: [cp().start() for cp in self.copies] and None)
+
+            def sent(self):
+                at_role(self.sender, lambda: [cp().wait_send() for cp in self.copies] and None)
+
+            def arrive(self):
+                def go():
+                    for cp in self.copies:
+                        cp().wait_recv()
+                    for h, at, m, parts in self.sums:
+                        add(h, at, m, parts)
+
+                at_role(self.receiver, go)
 
         k_send = take_send(3)
 
@@ -487,20 +501,33 @@
 
             lax.fori_loop(0, n // step, body, 0)
 
-        sends, adds, gathers = [], [], []
+        sums, back = [], []
+        holder = None
         off, n, both, stage = 0, nr, True, 0
+
+        def give_back(at, m, devs, **roles):
+            back.append(lambda src: Stage(
+                [
+                    copy(i, lambda: src(at, m), lambda: oreg(c, at, m), dev)
+                    for i, dev in enumerate(devs)
+                ],
+                **roles,
+            ))
+
         for step in route:
             if step == "y":
-                sends.append([copy(
-                    0, lambda off=off, n=n: greg(1 - f, off, n),
-                    lambda stage=stage, n=n: rreg(stage, 0, n), ypeer,
-                )])
-                adds.append([(f, off, n, [(stage, 0)])])
+                sums.append(Stage(
+                    [copy(
+                        0, lambda off=off, n=n: greg(1 - f, off, n),
+                        lambda stage=stage, n=n: rreg(stage, 0, n), ypeer,
+                    )],
+                    [(f, off, n, [(stage, 0)])],
+                ))
                 both = False
                 stage += 1
             elif step == "Z":
                 m4 = n // 4
-                out, parts, back = [], [], []
+                out, parts, devs = [], [], []
                 where = [(stage, 0), (stage, m4), (stage + 1, 0)]
                 mine_off = off + (2 * bits[1] + bits[2]) * m4
                 for i, (x1, x2) in enumerate(((0, 1), (1, 0), (1, 1))):
@@ -513,82 +540,98 @@
                         i, lambda to=to, m4=m4: greg(f, to, m4),
                         lambda st=st, at=at, m4=m4: rreg(st, at, m4), dev,
                     ))
-                    back.append(dev)
+                    devs.append(dev)
                     parts.append((st, at))
-                sends.append(out)
-                adds.append([(f, mine_off, m4, parts)])
-                gathers.append((mine_off, m4, back))
+                sums.append(Stage(out, [(f, mine_off, m4, parts)]))
+                give_back(mine_off, m4, devs)
                 off, n, stage = mine_off, m4, stage + 2
+            elif step == "E":
+                m2 = n // 2
+                inner = bits[1] + bits[2] - 2 * bits[1] * bits[2] == 1
+                outer = bits[1] + bits[2] - 2 * bits[1] * bits[2] == 0
+                middle = (d + (1 - 2 * bits[1]) * 4 + (1 - 2 * bits[2]) * 8, f)
+                keep, give = off + bits[2] * m2, off + (1 - bits[2]) * m2
+                sums.append(Stage(
+                    [copy(
+                        0, lambda off=off, n=n: greg(f, off, n),
+                        lambda stage=stage, n=n: rreg(stage, 0, n), peers[1],
+                    )],
+                    [(f, off, n, [(stage, 0)])], sender=outer, receiver=inner,
+                ))
+                sums.append(Stage(
+                    [copy(
+                        0, lambda give=give, m2=m2: greg(f, give, m2),
+                        lambda stage=stage, m2=m2: rreg(stage + 1, 0, m2), middle,
+                    )],
+                    [(f, keep, m2, [(stage + 1, 0)])], sender=inner, receiver=inner,
+                ))
+                give_back(off, n, [peers[1]], sender=inner, receiver=outer)
+                give_back(keep, m2, [middle], sender=inner, receiver=inner)
+                holder = inner
+                off, n, stage = keep, m2, stage + 2
             else:
                 j = int(step)
                 m2 = n // 2
                 give, keep = off + (1 - bits[j]) * m2, off + bits[j] * m2
                 owners = [0, 1] if both else [f]
-                sends.append([
-                    copy(
-                        i, lambda h=h, give=give, m2=m2: greg(h, give, m2),
-                        lambda stage=stage, i=i, m2=m2: rreg(stage, i * m2, m2), peers[j],
-                    )
-                    for i, h in enumerate(owners)
-                ])
-                adds.append([(h, keep, m2, [(stage, i * m2)]) for i, h in enumerate(owners)])
-                gathers.append((keep, m2, [peers[j]]))
+                sums.append(Stage(
+                    [
+                        copy(
+                            i, lambda h=h, give=give, m2=m2: greg(h, give, m2),
+                            lambda stage=stage, i=i, m2=m2: rreg(stage, i * m2, m2), peers[j],
+                        )
+                        for i, h in enumerate(owners)
+                    ],
+                    [(h, keep, m2, [(stage, i * m2)]) for i, h in enumerate(owners)],
+                ))
+                give_back(keep, m2, [peers[j]])
                 off, n, stage = keep, m2, stage + 1
         extra = [
             copy(
                 0, lambda off=off, n=n: greg(f, off, n),
-                lambda j=j, n=n: recv[4].at[j - 3, pl.ds((rbase >> 3), n), lanes], peers[j],
+                lambda j=j, n=n: recv[4].at[j - 3, pl.ds((rbase >> 2), n), lanes], peers[j],
             )
             for j in range(3, nbits)
         ]
         own = local(greg(f, off, n), oreg(c, off, n))
-        back = []
-        for depth, (at, m, devs) in enumerate(reversed(gathers)):
-            back.append([
-                copy(
-                    i,
-                    (lambda at=at, m=m: greg(f, at, m)) if depth == 0
-                    else (lambda at=at, m=m: oreg(c, at, m)),
-                    lambda at=at, m=m: oreg(c, at, m), dev,
-                )
-                for i, dev in enumerate(devs)
-            ])
-        back.append([copy(0, lambda: oreg(c, 0, nr), lambda: oreg(c, 0, nr), sib)])
-
-        def reduce_event(i):
-            for cp in sends[i]:
-                cp().wait_recv()
-            for h, at, m, parts in adds[i]:
-                add(h, at, m, parts)
-            if i + 1 < len(sends):
-                send(sends[i + 1], sends[i])
-                return
-            send((), sends[i])
+        gathers = [
+            make((lambda at, m: greg(f, at, m)) if i == 0 else (lambda at, m: oreg(c, at, m)))
+            for i, make in enumerate(reversed(back))
+        ]
+        gathers.append(Stage([copy(0, lambda: oreg(c, 0, nr), lambda: oreg(c, 0, nr), sib)]))
+
+        def finished():
             for m, cp in enumerate(extra):
-                send([cp])
-                send((), [cp])
+                cp().start()
+                cp().wait_send()
                 cp().wait_recv()
                 gr = greg(f, off, n)
                 gr[...] = (
                     gr[...].astype(F32)
-                    + recv[4][m, pl.ds((rbase >> 3), n), lanes].astype(F32)
+                    + recv[4][m, pl.ds((rbase >> 2), n), lanes].astype(F32)
                 ).astype(BF)
             own().start()
-            send(back[0])
+
+        def reduce_event(i):
+            sums[i].arrive()
+            sums[i].sent()
+            if i + 1 < len(sums):
+                sums[i + 1].start()
+                return
+            at_role(holder, finished)
+            gathers[0].start()
 
         def gather_event(i):
-            for cp in back[i]:
-                cp().wait_recv()
+            gathers[i].arrive()
             if i == 0:
-                own().wait()
-            if i + 1 < len(back):
-                send(back[i + 1], back[i])
-            else:
-                send((), back[i])
-
-        ch.start = lambda: send(sends[0])
-        ch.events = [functools.partial(reduce_event, i) for i in range(len(sends))] + [
-            functools.partial(gather_event, i) for i in range(len(back))
+                at_role(holder, lambda: own().wait())
+            gathers[i].sent()
+            if i + 1 < len(gathers):
+                gathers[i + 1].start()
+
+        ch.start = sums[0].start
+        ch.events = [functools.partial(reduce_event, i) for i in range(len(sums))] + [
+            functools.partial(gather_event, i) for i in range(len(gathers))
         ]
         chunks[name] = ch
 
@@ -849,8 +892,7 @@
             at = mo(h * D + 256 * k, 128)
             gd[pl.ds(at, 256), :] = dot(act[:, pl.ds(at, 256)], og[...], TN).astype(BF)
             for i in range(3):
-                early = ROUTES[f"d{i}"][0] == "y"
-                if early == (n == 0):
+                if n == 0 and ROUTES[f"d{i}"][0] == "y":
                     pl.when(k == i)(chunks[f"d{i}"].start)
             handle_at(k, {i: ("a", n, i) for i in range(3)})
             return carry
@@ -859,6 +901,9 @@
         lax.fori_loop(0, 3, down_grad, 0)
     zw_d(0).wait_recv()
     xw_d2().start()
+    for i in range(3):
+        if ROUTES[f"d{i}"][0] != "y":
+            chunks[f"d{i}"].start()
     l_wd().wait()
 
     for n in range(2):
@@ -1153,7 +1198,7 @@
     gq_h, go_h, gu_h, gd_h, out_h, clean_h, v_mask, v_ga, v_gm, v_bd, v_bu,
     b1, bd, fq, fo, fu, fd, bo, cg, ls,
 ):
-    L, D, NB = 384, 768, 4
+    L, D, NB = 384, 768, 8
     count = [0]
 
     def copy(src, dst):
@@ -1224,9 +1269,9 @@
         ((T, D), BF), ((T, D), F32), ((2 * T, D), BF), ((2 * T, L), BF), ((T, 128), F32),
         ((1536, D), BF), ((D, 3072), BF),
         ((D, D), BF), ((L, 3072), BF), ((L, D), BF), ((192, 3072), BF),
-        ((192, D), BF), ((96, 3072), BF), ((96, D), BF), ((48, 3072), BF),
-        ((nx, 96, D), BF) if nbits > 3 else ((1, 16, 128), BF),
-        ((nx, 48, 3072), BF) if nbits > 3 else ((1, 16, 128), BF),
+        ((L, D), BF), ((192, 3072), BF), ((192, D), BF), ((96, 3072), BF),
+        ((nx, 192, D), BF) if nbits > 3 else ((1, 16, 128), BF),
+        ((nx, 96, 3072), BF) if nbits > 3 else ((1, 16, 128), BF),
         ((nbits + 3, 8, D), F32), ((nbits + 3, 8, D), F32),
     ]
     block_out, clean_grad, fin, g1, gd = pl.pallas_call(
@@ -1273,7 +1318,7 @@
             pltpu.VMEM((L, 2304), F32), pltpu.VMEM((L, D), F32),
             pltpu.VMEM((L, 3072), F32), pltpu.VMEM((1536, D), F32),
             pltpu.VMEM((1, T, D), BF), pltpu.VMEM((1, L, D), F32),
-            pltpu.SemaphoreType.DMA((26,)),
+            pltpu.SemaphoreType.DMA((42,)),
         ],
         compiler_params=pltpu.CompilerParams(vmem_limit_bytes=64 * 2**20),
         name="finish",

time: 156 us -> 154 us (0.987)
  Pallas kernels: 155 us -> 153 us
    pallas_call x1, Pallas kernels: 144 us -> 142 us  [on_device(): pl.pallas_call(functools.partial(layer_kernel, nbits), out_shape=[jax.Sha...]
where the time goes in v4:
time: 154 us
  Pallas kernels  153 us (99%)
    pallas_call x1, Pallas kernels, on_device(): pl.pallas_call(functools.partial(layer_kernel, nbits), out_shape=[jax.Sha...  142 us
    pallas_call x1, Pallas kernels, on_device(): pl.pallas_call(finish_kernel, out_shape=[jax.ShapeDtypeStruct((L, 2304),...  10.9 us

profile of v4, /device:TPU:1, one launch (start us, length us, event | category | flops | bytes accessed | tf_op | source)
XLA Modules:
  0.0 153.9 jit_solution(4092384288971229138)
XLA Ops:
  0.6 142.1 %layer.1 = (bf16[1,768,768]{2,1,0:T(8,128)(2,1)}, f32[1,384,768]{2,1,0:T(8,128)}, f32[8,384]{1,0:T(8,128)}, bf16[2,384,3072]{2,1,0:T(8,128)(2,1)}, bf16[2,768,768]{2,1,0:T(8,128)(2,1)}) custom-call(bf16[1,384,768]{2,1,0:T(8,128)(2,1)} %clean_h.1, s32[1,384]{1,0:T(1,128)} %noise.1, bf16[384]{0:T(512)(128)(2,1)} %v_mask.1, bf16[384]{0:T(512)(128)(2,1)} %v_ga.1, ...), custom_call_target="tpu_custom_call" | custom-call | tf_op jit(solution)/shard_map/layer/pallas_call | solution.py:1277
  142.8 10.9 %finish.1 = (f32[384,2304]{1,0:T(8,128)}, f32[384,768]{1,0:T(8,128)}, f32[384,3072]{1,0:T(8,128)}, f32[1536,768]{1,0:T(8,128)}, bf16[1,768,768]{2,1,0:T(8,128)(2...) custom-call(bf16[2,384,3072]{2,1,0:T(8,128)(2,1)} %get-tuple-element, ...), custom_call_target="tpu_custom_call" | custom-call | tf_op jit(solution)/shard_map/finish/pallas_call | solution.py:1303

commit v5 on v4

--- a/solution.py
+++ b/solution.py
@@ -18,7 +18,7 @@
 F32 = jnp.float32
 MESH = pl.DeviceIdType.MESH
 LOGIT_SCALE = 0.125 * math.log2(math.e)
-N_SEND, N_RECV, N_LOCAL = 102, 185, 38
+N_SEND, N_RECV, N_LOCAL = 93, 185, 38
 NN = (((1,), (0,)), ((), ()))
 NT = (((1,), (1,)), ((), ()))
 TN = (((0,), (0,)), ((), ()))
@@ -478,7 +478,7 @@
 
                 at_role(self.receiver, go)
 
-        k_send = take_send(3)
+        k_send = take_send(3 if "Z" in route else 1 if route[0] == "y" else 2)
 
         def copy(i, src, dst, dev):
             k = take_recv()
@@ -850,15 +850,14 @@
     lax.fori_loop(0, NT3, out_proj, 0)
     for h in range(2):
         l_wu[h]().wait()
+    w_u(1)
     w_u_end(0)
-    w_u(1)
 
     for n in range(2):
         h = half_of(n)
         lanes = up_lanes(n)
         if n == 1:
             w_u_end(1)
-            w_d(0)
         bu = jnp.concatenate(
             [small[h, pl.ds(4 + 2 * c + r, 1), :] for r in range(2)], axis=1
         )
@@ -885,6 +884,7 @@
         lax.fori_loop(0, 4, rows_a, 0)
         if n == 0:
             s_og().wait_recv()
+            w_d(0)
         else:
             w_d(1)
 
@@ -1198,7 +1198,7 @@
     gq_h, go_h, gu_h, gd_h, out_h, clean_h, v_mask, v_ga, v_gm, v_bd, v_bu,
     b1, bd, fq, fo, fu, fd, bo, cg, ls,
 ):
-    L, D, NB = 384, 768, 8
+    L, D, NB = 384, 768, 4
     count = [0]
 
     def copy(src, dst):
@@ -1318,7 +1318,7 @@
             pltpu.VMEM((L, 2304), F32), pltpu.VMEM((L, D), F32),
             pltpu.VMEM((L, 3072), F32), pltpu.VMEM((1536, D), F32),
             pltpu.VMEM((1, T, D), BF), pltpu.VMEM((1, L, D), F32),
-            pltpu.SemaphoreType.DMA((42,)),
+            pltpu.SemaphoreType.DMA((26,)),
         ],
         compiler_params=pltpu.CompilerParams(vmem_limit_bytes=64 * 2**20),
         name="finish",

time: 154 us -> 154 us (level)
  no operation moved by 1% of the time
where the time goes in v5:
time: 154 us
  Pallas kernels  153 us (99%)
    pallas_call x1, Pallas kernels, on_device(): pl.pallas_call(functools.partial(layer_kernel, nbits), out_shape=[jax.Sha...  142 us
    pallas_call x1, Pallas kernels, on_device(): pl.pallas_call(finish_kernel, out_shape=[jax.ShapeDtypeStruct((L, 2304),...  10.8 us

profile of v5, /device:TPU:1, one launch (start us, length us, event | category | flops | bytes accessed | tf_op | source)
XLA Modules:
  0.0 154.0 jit_solution(15070402348359784089)
XLA Ops:
  0.6 142.3 %layer.1 = (bf16[1,768,768]{2,1,0:T(8,128)(2,1)}, f32[1,384,768]{2,1,0:T(8,128)}, f32[8,384]{1,0:T(8,128)}, bf16[2,384,3072]{2,1,0:T(8,128)(2,1)}, bf16[2,768,768]{2,1,0:T(8,128)(2,1)}) custom-call(bf16[1,384,768]{2,1,0:T(8,128)(2,1)} %clean_h.1, s32[1,384]{1,0:T(1,128)} %noise.1, bf16[384]{0:T(512)(128)(2,1)} %v_mask.1, bf16[384]{0:T(512)(128)(2,1)} %v_ga.1, ...), custom_call_target="tpu_custom_call" | custom-call | tf_op jit(solution)/shard_map/layer/pallas_call | solution.py:1277
  143.0 10.8 %finish.1 = (f32[384,2304]{1,0:T(8,128)}, f32[384,768]{1,0:T(8,128)}, f32[384,3072]{1,0:T(8,128)}, f32[1536,768]{1,0:T(8,128)}, bf16[1,768,768]{2,1,0:T(8,128)(2...) custom-call(bf16[2,384,3072]{2,1,0:T(8,128)(2,1)} %get-tuple-element, ...), custom_call_target="tpu_custom_call" | custom-call | tf_op jit(solution)/shard_map/finish/pallas_call | solution.py:1303
